TPU v7x, 32 devices: a whole 2x2x4 slice. The times are simulated.
32 devices in a mesh: scen: 4 (over y, x), gx: 2 (over core), gy: 4 (over z).
Axes of the slice: x: 2, y: 2, z: 4, core: 2. Of those that a mesh axis runs over, the one named last changes fastest.
Arguments:
- perm_log: float32 [2, 128, 512], P(None, 'gx', 'gy'), may hold values from -2.5 to 2.5
- facies: int32 [2, 128, 512], P(None, 'gx', 'gy'), may hold values from 0 to 3
- facies_scale: float32 [4], replicated, may hold values from 0.5 to 2
- accumulation: float32 [2, 128, 512], P(None, 'gx', 'gy'), may hold values from 0.05 to 0.5
- previous_pressure: float32 [4, 2, 128, 512], P('scen', None, 'gx', 'gy'), may hold values from -6 to 6
- observed: float32 [4, 2, 128, 512], P('scen', None, 'gx', 'gy'), may hold values from -6 to 6
- well_cells: int32 [4, 5], P('scen'), may hold values from 0 to 131071
- well_rates: float32 [4, 5], P('scen'), may hold values from 5 to 20
Outputs:
- pressure: float32 [4, 2, 128, 512], P('scen', None, 'gx', 'gy')
- adjoint: float32 [4, 2, 128, 512], P('scen', None, 'gx', 'gy')
- gradient: float32 [2, 128, 512], P(None, 'gx', 'gy')
Inputs may be any that keep to these rules, and one draw needn't show every extreme that they name: `well_cells`: a flat index layer * 128 * 512 + row * 512 + column of a grid cell; several wells may share a cell.
All inputs are finite; a program needn't handle non-finite values.
Results may differ from a plain program's by a relative error of at most 0.0001.
Values sent between devices are 32-bit elements; how exact they have to be, the bound alone decides.
No kernel may reach another device: no remote copies, remote signals or barrier semaphores. Data moves between devices by JAX's collectives and lax.ppermute only.
A program may use at most 128 MiB of HBM per device.

v0:
```python
from functools import partial

import jax
import jax.numpy as jnp
from jax import lax
from jax.experimental import pallas as pl
from jax.experimental.pallas import tpu as pltpu
from jax.sharding import PartitionSpec as P

WELLS = 5
FACIES = 4
LAYERS = 2
SMOOTH = 2
COARSE = 4

vertical = 0.3
damping = 0.8

LANES = 128
HALF = 64
SUB = 8
PERM, ACC, PREV, OBS = range(4)
NEAR = 26
ROOM = HALF // 2 - NEAR
LEVELS = ((2, 1), (1, 1), (1, 2))


def lane_index():
    return lax.broadcasted_iota(jnp.int32, (SUB, LANES), 1)


def row_index():
    return lax.broadcasted_iota(jnp.int32, (SUB, LANES), 0)


def lane_roll(value, shift):
    return pltpu.roll(value, shift % LANES, value.ndim - 1)


def row_roll(value, shift):
    return pltpu.roll(value, shift % SUB, 0)


def shuffle(value, inverse):
    rows = lax.broadcasted_iota(jnp.int32, (LANES, LANES), 0)
    cols = lax.broadcasted_iota(jnp.int32, (LANES, LANES), 1)
    natural, place = (cols, rows) if inverse else (rows, cols)
    matrix = (natural == 2 * (place % HALF) + place // HALF).astype(jnp.bfloat16)
    rest = value.reshape(-1, LANES)
    total = None
    for _ in range(3):
        part = rest.astype(jnp.bfloat16)
        rest = rest - part.astype(jnp.float32)
        moved_part = jnp.dot(part, matrix, preferred_element_type=jnp.float32)
        total = moved_part if total is None else total + moved_part
    return total.reshape(value.shape)


def place_in_half(shape):
    return lax.broadcasted_iota(jnp.int32, shape, len(shape) - 1) % HALF


def spare_lanes(number, place):
    shift = NEAR - number * ROOM
    low, high = number * ROOM, HALF - (number + 1) * ROOM
    return (((place >= NEAR) & (place < HALF // 2), (place >= low) & (place < low + ROOM), shift),
            ((place >= HALF // 2) & (place < HALF - NEAR), (place >= high) & (place < high + ROOM), -shift))


def interleaved(rows):
    count = rows.shape[0] // SUB
    return jnp.concatenate([rows[pl.ds(t, SUB, stride=count), :] for t in range(count)], axis=0)


def put_in_order(shuffled, ordered):
    count = ordered.shape[-2] // SUB
    natural = shuffle(shuffled, True)
    for layer in range(LAYERS):
        for t in range(count):
            ordered[layer, pl.ds(t, SUB, stride=count), :] = natural[layer, t * SUB:(t + 1) * SUB]


def pack_kernel(scale_hbm, perm_log_hbm, facies_hbm, acc_hbm, prev_hbm, obs_hbm, own, message_a, message_b,
                scale, perm_log, facies, acc, prev, obs, sems):
    pairs = ((scale_hbm, scale), (perm_log_hbm, perm_log), (facies_hbm, facies), (acc_hbm, acc), (prev_hbm, prev),
             (obs_hbm, obs))
    copies = [pltpu.make_async_copy(source, target, sems.at[i]) for i, (source, target) in enumerate(pairs)]
    for copy in copies:
        copy.start()
    for copy in copies:
        copy.wait()

    def layers(ref):
        return jnp.stack([interleaved(ref.at[layer]) for layer in range(LAYERS)])

    label = layers(facies)
    factor = jnp.zeros(label.shape, jnp.float32)
    for number in range(FACIES):
        factor = factor + jnp.where(label == number, scale[number], jnp.float32(0.0))
    fields = [shuffle(value, False) for value in (jnp.exp(layers(perm_log)) * factor, layers(acc), layers(prev.at[0]), layers(obs.at[0]))]
    for number in range(4):
        own[number] = fields[number]
    place = place_in_half(label.shape)
    full = []
    for number in range(3):
        value = fields[number]
        for lanes, _, shift in spare_lanes(number, place):
            value = jnp.where(lanes, lane_roll(fields[OBS], shift), value)
        full.append(value)
    low = place_in_half(label.shape[1:]) < HALF // 2
    left_first = low == (lax.axis_index("gy") % 2 == 1)
    couples = [(full[0][layer], full[1][layer]) for layer in range(LAYERS)] + [(full[2][0], full[2][1])]
    for plane, (one, two) in enumerate(couples):
        first, second = lane_roll(one, HALF), lane_roll(two, HALF + HALF // 2)
        message_a[plane] = jnp.where(left_first, first, second)
        message_b[plane] = jnp.where(left_first, second, first)


def merge_kernel(message_a, message_b, beside):
    place = place_in_half(beside.shape[2:])
    from_a = (place < HALF // 2) != (lax.axis_index("gy") % 2 == 1)
    full = [[], [], []]
    for plane in range(3):
        a, b = message_a[plane], message_b[plane]
        one = jnp.where(from_a, a, b)
        two = lane_roll(jnp.where(from_a, b, a), -(HALF // 2))
        for number, value in zip((0, 1) if plane < 2 else (2, 2), (one, two)):
            full[number].append(value)
    near = (place < NEAR) | (place >= HALF - NEAR)
    for layer in range(LAYERS):
        observed = jnp.zeros(place.shape, jnp.float32)
        for number in range(3):
            value = full[number][layer]
            beside[number, layer] = jnp.where(near, value, 0.0)
            for _, lanes, shift in spare_lanes(number, place):
                observed = jnp.where(lanes, lane_roll(value, -shift), observed)
        beside[OBS, layer] = observed


class Level:
    def __init__(self, count, width, span, blocks, refs):
        self.count = count
        self.width = width
        self.span = span
        self.blocks = blocks
        (self.c_south, self.c_first, self.c_inner, self.c_east, self.c_west, self.c_layer, self.weight, self.diag,
         self.target, self.now, self.later) = refs

    @staticmethod
    def scratch(count, width, blocks):
        def vectors(*lead):
            return pltpu.VMEM(lead + (SUB, LANES), jnp.float32)

        whole = vectors(LAYERS, width, blocks, count)
        edge = vectors(LAYERS, blocks, count)
        return [whole, vectors(LAYERS, width, blocks), edge, edge, edge, vectors(width, blocks, count)] + [whole] * 5

    def steps(self):
        for b in range(self.blocks):
            for t in range(self.count):
                yield b, t

    def members(self):
        for layer in range(LAYERS):
            for u in range(self.width):
                yield layer, u


def row_before(values):
    edge = row_index() < 1
    rolled = [row_roll(value, 1) for value in values]
    return [jnp.where(edge, rolled[b - 1], rolled[b]) for b in range(len(values))]


def row_after(values):
    edge = row_index() >= SUB - 1
    rolled = [row_roll(value, -1) for value in values]
    return [jnp.where(edge, rolled[(b + 1) % len(values)], rolled[b]) for b in range(len(values))]


class Field:
    def __init__(self, level, source, coarse=None):
        self.source = source
        self.coarse = coarse
        self.count = level.count
        self.read = {}
        self.before, self.after = {}, {}
        for layer, u in level.members():
            lows = row_before([self.value(layer, u, b, level.count - 1) for b in range(level.blocks)])
            highs = row_after([self.value(layer, u, b, 0) for b in range(level.blocks)])
            for b in range(level.blocks):
                self.before[layer, u, b] = lows[b]
                self.after[layer, u, b] = highs[b]

    def value(self, layer, u, b, t):
        value = self.source[layer, u, b, t]
        return value if self.coarse is None else value + self.coarse[layer, 0, b, t // 2]

    def at(self, layer, u, b, t):
        if t < 0:
            return self.before[layer, u, b]
        if t >= self.count:
            return self.after[layer, u, b]
        key = layer, u, b, t
        if key not in self.read:
            self.read[key] = self.value(*key)
        return self.read[key]


def row_coeff(level, layer, u, b, t):
    return level.c_south[layer, u, b, t] if t >= 0 else level.c_first[layer, u, b]


def neighbour_sums(level, source, coarse=None):
    field = Field(level, source, coarse)
    coeffs = {}
    for b, t in level.steps():
        for member in level.members():
            for at in (t - 1, t):
                if (member, b, at) not in coeffs:
                    coeffs[member, b, at] = row_coeff(level, *member, b, at)
        layer_coeffs = [level.c_layer[u, b, t] for u in range(level.width)]
        for layer in range(LAYERS):
            here = [field.at(layer, u, b, t) for u in range(level.width)]
            east_coeff, west_coeff = level.c_east[layer, b, t], level.c_west[layer, b, t]
            if level.width == 2:
                inner = level.c_inner[layer, b, t]
                beside = [inner * here[1] + west_coeff * lane_roll(here[1], 1),
                          inner * here[0] + east_coeff * lane_roll(here[0], -1)]
            else:
                beside = [east_coeff * lane_roll(here[0], -level.span) + west_coeff * lane_roll(here[0], level.span)]
            for u in range(level.width):
                total = (coeffs[(layer, u), b, t - 1] * field.at(layer, u, b, t - 1)
                         + coeffs[(layer, u), b, t] * field.at(layer, u, b, t + 1)
                         + (beside[u] + layer_coeffs[u] * field.at(1 - layer, u, b, t)))
                yield (layer, u, b, t), here[u], total


def sweep(level, source, result, coarse=None):
    for key, value, total in neighbour_sums(level, source, coarse):
        result[key] = (1.0 - damping) * value + level.weight[key] * (level.target[key] + total)


def sweeps(level, count, coarse=None):
    for number in range(count):
        sweep(level, level.now, level.later, coarse if number == 0 else None)
        level.now, level.later = level.later, level.now


def first_sweep(level):
    for b, t in level.steps():
        for layer, u in level.members():
            key = layer, u, b, t
            level.now[key] = level.weight[key] * level.target[key]


def pair_sum(value, span):
    lower = lane_index() % (2 * span) < span
    return value + jnp.where(lower, lane_roll(value, -span), lane_roll(value, span))


def low_group(value, span):
    return jnp.where(lane_index() % (2 * span) < span, value, lane_roll(value, span))


def high_group(value, span):
    return jnp.where(lane_index() % (2 * span) < span, lane_roll(value, -span), value)


def column_sum(values, level):
    return values[0] + values[1] if level.width == 2 else pair_sum(values[0], level.span)


def restrict_residual(fine, coarse):
    residuals = {}
    for key, value, total in neighbour_sums(fine, fine.now):
        layer, u, b, t = key
        residuals[key] = fine.target[key] + total - fine.diag[key] * value
        if t % 2 == 1 and u == fine.width - 1:
            rows = [residuals[layer, v, b, t - 1] + residuals[layer, v, b, t] for v in range(fine.width)]
            coarse.target[layer, 0, b, t // 2] = column_sum(rows, fine)


def vcycle(levels):
    finest, middle, bottom = levels
    sweeps(finest, SMOOTH - 1)
    restrict_residual(finest, middle)
    first_sweep(middle)
    sweeps(middle, SMOOTH - 1)
    restrict_residual(middle, bottom)
    first_sweep(bottom)
    sweeps(bottom, COARSE - 1)
    sweeps(middle, SMOOTH, bottom.now)
    sweeps(finest, SMOOTH, middle.now)


def harmonic(left, right):
    return 2.0 * left * right / jnp.maximum(left + right, 1e-20)


def finest_coeffs(level, perm, joined):
    last = level.count - 1
    for layer, u in level.members():
        heads = [perm[layer, u, b, 0] for b in range(level.blocks)]
        rolled = [row_roll(value, -1) for value in heads]
        edge = row_index() >= SUB - 1
        for b in range(level.blocks):
            after = jnp.where(edge, joined[b] * rolled[(b + 1) % level.blocks], rolled[b])
            for t in range(level.count):
                beyond = perm[layer, u, b, t + 1] if t < last else after
                level.c_south[layer, u, b, t] = harmonic(perm[layer, u, b, t], beyond)
        firsts = row_before([level.c_south[layer, u, b, last] for b in range(level.blocks)])
        for b in range(level.blocks):
            level.c_first[layer, u, b] = firsts[b]
    for b, t in level.steps():
        for u in range(level.width):
            level.c_layer[u, b, t] = vertical * harmonic(perm[0, u, b, t], perm[1, u, b, t])
        for layer in range(LAYERS):
            even, odd = perm[layer, 0, b, t], perm[layer, 1, b, t]
            level.c_inner[layer, b, t] = harmonic(even, odd)
            east = harmonic(odd, lane_roll(even, -1))
            level.c_east[layer, b, t] = east
            level.c_west[layer, b, t] = lane_roll(east, 1)


def with_weight(level, acc):
    for b, t in level.steps():
        for layer, u in level.members():
            key = layer, u, b, t
            if level.width == 2:
                beside = level.c_inner[layer, b, t] + (level.c_west, level.c_east)[u][layer, b, t]
            else:
                beside = level.c_west[layer, b, t] + level.c_east[layer, b, t]
            diag = (row_coeff(level, layer, u, b, t - 1) + row_coeff(level, layer, u, b, t)
                    + (beside + level.c_layer[u, b, t]) + acc[key])
            level.diag[key] = diag
            level.weight[key] = damping / jnp.maximum(diag, 1e-20)


def coarse_coeffs(fine, coarse, fine_acc, coarse_acc):
    width = range(fine.width)
    for b in range(coarse.blocks):
        for layer in range(LAYERS):
            coarse.c_first[layer, 0, b] = column_sum([fine.c_first[layer, u, b] for u in width], fine)
    for b, t in coarse.steps():
        one, two = 2 * t, 2 * t + 1
        coarse.c_layer[0, b, t] = column_sum([fine.c_layer[u, b, one] + fine.c_layer[u, b, two] for u in width], fine)
        for layer in range(LAYERS):
            coarse.c_south[layer, 0, b, t] = column_sum([fine.c_south[layer, u, b, two] for u in width], fine)
            coarse_acc[layer, 0, b, t] = column_sum(
                [fine_acc[layer, u, b, one] + fine_acc[layer, u, b, two] for u in width], fine)
            west = fine.c_west[layer, b, one] + fine.c_west[layer, b, two]
            east = fine.c_east[layer, b, one] + fine.c_east[layer, b, two]
            if fine.width == 1:
                west, east = low_group(west, fine.span), high_group(east, fine.span)
            coarse.c_west[layer, b, t] = west
            coarse.c_east[layer, b, t] = east
    with_weight(coarse, coarse_acc)


def own_columns(even, odd):
    return jnp.where(lane_index() < HALF, even, lane_roll(odd, HALF))


def face_terms(level, pressure, adjoint, perm):
    def face(coeff, one, two):
        changes = [field.at(*one) - (field.at(*two) if isinstance(two, tuple) else two[number])
                   for number, field in enumerate((pressure, adjoint))]
        return (coeff * coeff) * (changes[0] * changes[1])

    rows = {(layer, u): face(level.c_first[layer, u, 0], (layer, u, 0, -1), (layer, u, 0, 0))
            for layer, u in level.members()}
    for t in range(level.count):
        between = [(1.0 / vertical) * face(level.c_layer[u, 0, t], (0, u, 0, t), (1, u, 0, t)) for u in range(2)]
        for layer in range(LAYERS):
            inner = face(level.c_inner[layer, 0, t], (layer, 0, 0, t), (layer, 1, 0, t))
            easts = [lane_roll(field.at(layer, 0, 0, t), -1) for field in (pressure, adjoint)]
            east = face(level.c_east[layer, 0, t], (layer, 1, 0, t), easts)
            terms = []
            for u in range(2):
                south = face(level.c_south[layer, u, 0, t], (layer, u, 0, t), (layer, u, 0, t + 1))
                beside = lane_roll(east, 1) if u == 0 else east
                total = rows[layer, u] + south + (inner + beside) + between[u]
                rows[layer, u] = south
                terms.append(-0.5 * total / perm[layer, u, 0, t])
            yield layer, t, own_columns(*terms)


def order_kernel(*refs):
    for shuffled, ordered in zip(refs[:2], refs[2:]):
        put_in_order(shuffled[...], ordered.at[0])


def cycle_kernel(grid_shape, blocks, *refs):
    cells_hbm, rates_hbm = refs[:2]
    inputs = [refs[2 + 2 * b:4 + 2 * b] for b in range(blocks)]
    refs = refs[2 + 2 * blocks:]
    pressure_out, adjoint_out, terms_out = refs[:3]
    cells, rates, sems, perm, acc, middle_acc, bottom_acc, states, terms_rows = refs[3:12]
    refs = refs[12:]
    copies = [pltpu.make_async_copy(cells_hbm, cells, sems.at[0]), pltpu.make_async_copy(rates_hbm, rates, sems.at[1])]
    for copy in copies:
        copy.start()
    count = inputs[0][0].shape[2] // SUB
    levels = [Level(count >> depth, width, span, blocks, refs[11 * depth:11 * depth + 11])
              for depth, (width, span) in enumerate(LEVELS)]
    finest, middle, bottom = levels

    def rows(t):
        return pl.ds(t * SUB, SUB)

    def fields(number, layer, b, t):
        low = lane_index() < HALF
        own, beside = [value[number, layer, rows(t), :] for value in inputs[b]]
        return jnp.where(low, own, beside), lane_roll(jnp.where(low, beside, own), HALF)

    gx = lax.axis_index("gx")
    if blocks == 3:
        joined = [1.0, 0.0, 1.0]
    elif blocks == 2:
        joined = [1.0 - gx.astype(jnp.float32), gx.astype(jnp.float32)]
    else:
        joined = [0.0]

    for b, t in finest.steps():
        for layer in range(LAYERS):
            perms, accs, starts = [fields(number, layer, b, t) for number in (PERM, ACC, PREV)]
            for u in range(2):
                key = layer, u, b, t
                perm[key] = perms[u]
                acc[key] = accs[u]
                finest.now[key] = starts[u]
                finest.target[key] = accs[u] * starts[u]

    for copy in copies:
        copy.wait()
    layer_count, total_rows, total_cols = grid_shape
    block_rows, block_cols = SUB * count, LANES
    for well in range(WELLS):
        cell = cells[0, well]
        layer = cell // (total_rows * total_cols)
        row = cell // total_cols % total_rows - gx * block_rows
        col = cell % total_cols - lax.axis_index("gy") * block_cols
        if blocks == 3:
            row_inside = (row >= -block_rows) & (row < 2 * block_rows)
        elif blocks == 2:
            row_inside = row >= -block_rows
        else:
            row_inside = row >= 0
        inside = row_inside & (col >= -HALF) & (col < block_cols + HALF)
        row = jnp.where(row < 0, row + blocks * block_rows, row)
        col = jnp.where(col < 0, col + 2 * block_cols, col)
        row = jnp.where(inside, row, 0)
        col = jnp.where(inside, col, 0)
        rate = jnp.where(inside, rates[0, well], 0.0)
        in_block = row % block_rows
        place = layer, col % 2, row // block_rows, in_block % count
        hit = (row_index() == in_block // count) & (lane_index() == col // 2)
        finest.target[place] = finest.target[place] + jnp.where(hit, rate, 0.0)

    finest_coeffs(finest, perm, joined)
    with_weight(finest, acc)
    coarse_coeffs(finest, middle, acc, middle_acc)
    coarse_coeffs(middle, bottom, middle_acc, bottom_acc)

    sweeps(finest, 1)
    start, other = finest.now, finest.later

    def turn(number, carry):
        finest.now, finest.later = start, other
        vcycle(levels)
        for b, t in finest.steps():
            for layer in range(LAYERS):
                observed = fields(OBS, layer, b, t)
                for u in range(2):
                    key = layer, u, b, t
                    value = finest.now[key]
                    states[(number,) + key] = value
                    target = value - observed[u]
                    finest.target[key] = target
                    start[key] = finest.weight[key] * target
        return carry

    lax.fori_loop(0, 2, turn, 0)
    pressure, adjoint = states.at[0], states.at[1]
    for t in range(count):
        for layer in range(LAYERS):
            for state, result in ((pressure, pressure_out), (adjoint, adjoint_out)):
                result[layer, rows(t), :] = own_columns(*[state[layer, u, 0, t] for u in range(2)])

    for layer, t, terms in face_terms(finest, Field(finest, pressure), Field(finest, adjoint), perm):
        terms_rows[layer, rows(t), :] = terms
    put_in_order(terms_rows[...], terms_out)


def moved(value, axis, step):
    count = lax.axis_size(axis)
    ring = axis == "gx" and count == 2
    pairs = [((i + step) % count, i) for i in range(count) if ring or 0 <= i + step < count]
    return lax.ppermute(value, axis, pairs)


def swapped(value, axis, first):
    pairs = []
    for i in range(first, lax.axis_size(axis) - 1, 2):
        pairs += [(i, i + 1), (i + 1, i)]
    return lax.ppermute(value, axis, pairs)


def summed(value, axis):
    count = lax.axis_size(axis)
    others = [lax.ppermute(value, axis, [(i, i ^ step) for i in range(count)]) for step in range(count - 1, 0, -1)]
    terms = [value] + others[::-1]
    while len(terms) > 1:
        terms = [terms[i] + terms[i + 1] for i in range(0, len(terms), 2)]
    return terms[0]


def in_hbm(value):
    return pltpu.with_memory_space_constraint(value, pltpu.HBM)


def in_vmem(value):
    return pltpu.with_memory_space_constraint(value, pltpu.VMEM)


def shards(
    perm_log,
    facies,
    facies_scale,
    accumulation,
    previous_pressure,
    observed,
    well_cells,
    well_rates,
):
    layer_count, row_count, col_count = perm_log.shape
    gx_count, gy_count = lax.axis_size("gx"), lax.axis_size("gy")
    vmem = pl.BlockSpec(memory_space=pltpu.VMEM)
    hbm = pl.BlockSpec(memory_space=pltpu.HBM)
    f32 = jnp.float32
    fields = (perm_log, facies, accumulation, previous_pressure, observed)
    block = (layer_count, row_count, col_count)
    own, message_a, message_b = pl.pallas_call(
        pack_kernel,
        out_shape=[
            pltpu.VMEM((4,) + block, f32),
            pltpu.VMEM((3,) + block[1:], f32),
            pltpu.VMEM((3,) + block[1:], f32),
        ],
        in_specs=[hbm] * 6,
        out_specs=[vmem] * 3,
        scratch_shapes=[pltpu.SMEM(facies_scale.shape, f32)]
        + [pltpu.VMEM(value.shape, value.dtype) for value in fields] + [pltpu.SemaphoreType.DMA((6,))],
        name="pack",
    )(in_hbm(facies_scale), *[in_hbm(value) for value in fields])

    steps = (0, 1) if gx_count == 2 else (0, 1, -1) if gx_count > 2 else (0,)
    blocks = len(steps)
    owns = [own] + [moved(own, "gx", step) for step in steps[1:]]
    merge = pl.pallas_call(
        merge_kernel,
        out_shape=pltpu.VMEM((4,) + block, f32),
        in_specs=[vmem] * 2,
        out_specs=vmem,
        cost_estimate=pl.CostEstimate(flops=2**20, bytes_accessed=2**19, transcendentals=0),
        name="merge",
    )
    messages = swapped(message_a, "gy", 0), swapped(message_b, "gy", 1)
    besides = [merge(*[in_vmem(value) for value in messages])]
    for step in steps[1:]:
        besides.append(merge(*[in_vmem(moved(value, "gx", step)) for value in messages]))
    operands = [in_vmem(value) for pair in zip(owns, besides) for value in pair]

    count = row_count // SUB
    scratch = [pltpu.SMEM(well_cells.shape, jnp.int32), pltpu.SMEM(well_rates.shape, f32), pltpu.SemaphoreType.DMA((2,))]
    whole = [pltpu.VMEM((LAYERS, width, blocks, count >> depth, SUB, LANES), f32) for depth, (width, _) in enumerate(LEVELS)]
    scratch += [whole[0], whole[0], whole[1], whole[2]]
    scratch += [pltpu.VMEM((2, LAYERS, 2, blocks, count, SUB, LANES), f32), pltpu.VMEM(block, f32)]
    for depth, (width, _) in enumerate(LEVELS):
        scratch += Level.scratch(count >> depth, width, blocks)
    state = jax.ShapeDtypeStruct((1, layer_count, row_count, col_count), f32)
    grid_shape = (layer_count, row_count * gx_count, col_count * gy_count)
    *shuffled, terms = pl.pallas_call(
        partial(cycle_kernel, grid_shape, blocks),
        out_shape=[pltpu.VMEM(block, f32)] * 3,
        in_specs=[hbm] * 2 + [vmem] * (2 * blocks),
        out_specs=[vmem] * 3,
        scratch_shapes=scratch,
        compiler_params=pltpu.CompilerParams(vmem_limit_bytes=24 * 1024 * 1024),
        name="cycles",
    )(in_hbm(well_cells), in_hbm(well_rates), *operands)
    gradient = summed(terms, "scen")
    pressure, adjoint = pl.pallas_call(
        order_kernel,
        out_shape=[state] * 2,
        in_specs=[vmem] * 2,
        out_specs=[vmem] * 2,
        cost_estimate=pl.CostEstimate(flops=2 * row_count * LANES**2 * 16, bytes_accessed=2**19, transcendentals=0),
        name="order",
    )(*[in_vmem(value) for value in shuffled])
    return pressure, adjoint, gradient


def solution(mesh):
    return jax.shard_map(
        shards,
        mesh=mesh,
        in_specs=(
            P(None, "gx", "gy"),
            P(None, "gx", "gy"),
            P(),
            P(None, "gx", "gy"),
            P("scen", None, "gx", "gy"),
            P("scen", None, "gx", "gy"),
            P("scen", None),
            P("scen", None),
        ),
        out_specs=(P("scen", None, "gx", "gy"), P("scen", None, "gx", "gy"), P(None, "gx", "gy")),
        check_vma=False,
    )
```

profile of v0, /device:TPU:16, one launch (start us, length us, event | category | flops | bytes accessed | tf_op | source)
XLA Modules:
  0.0 24.0 jit_solution(17835897410855290593)
XLA Ops:
  0.6 1.5 %pack.1 = (f32[4,2,64,128]{3,2,1,0:T(8,128)S(1)}, f32[3,64,128]{2,1,0:T(8,128)S(1)}, f32[3,64,128]{2,1,0:T(8,128)S(1)}) custom-call(f32[4]{0:T(128)} %scale_hbm.1, f32[2,64,128]{2,1,0:T(8,128)} %perm_log_hbm.1, s32[2,64,128]{2,1,0:T(8,128)} %facies_hbm.1, f32[2,64,128]{2,1,0:T(8,128)} %acc_hbm.1, f32[1,2,64,128]{3,2,1,0:T(8,128)} %prev_hbm.1, ...), custom_call_target="tpu_custom_call" | custom-call | tf_op jit(solution)/shard_map/pack/pallas_call | solution.py:544
  2.1 0.1 collective-permute-start.2
  2.2 1.6 %collective-permute-start = (f32[3,64,128]{2,1,0:T(8,128)S(1)}, f32[3,64,128]{2,1,0:T(8,128)S(1)}, u32[]{:S(2)}, u32[]{:S(2)}) collective-permute-start(f32[3,64,128]{2,1,0:T(8,128)S(1)} %get-tuple-element.12), channel_id=1, source_target_pairs={{0,1},{1,0},{2,3},{3,2},{4,5},{5,4},{6,7},{7,6},{8,9},{9,8},{10,11... | collective-permute-start | bytes 294920 | tf_op jit(solution)/shard_map/ppermute | solution.py:507
  3.8 1.9 %collective-permute-start.1 = (f32[3,64,128]{2,1,0:T(8,128)S(1)}, f32[3,64,128]{2,1,0:T(8,128)S(1)}, u32[]{:S(2)}, u32[]{:S(2)}) collective-permute-start(f32[3,64,128]{2,1,0:T(8,128)S(1)} %get-tuple-element.13), channel_id=1, source_target_pairs={{1,2},{2,1},{5,6},{6,5},{9,10},{10,9},{13,14},{14,13},{17,18},{18,... | collective-permute-start | bytes 294920 | tf_op jit(solution)/shard_map/ppermute | solution.py:507
  5.8 1.7 %collective-permute-done.message_a = f32[3,64,128]{2,1,0:T(8,128)S(1)} collective-permute-done((f32[3,64,128]{2,1,0:T(8,128)S(1)}, f32[3,64,128]{2,1,0:T(8,128)S(1)}, u32[]{:S(2)}, u32[]{:S(2)}) %collective-permute-start) | collective-permute-done | bytes 98336 | tf_op jit(solution)/shard_map/ppermute | solution.py:507
  7.4 0.0 collective-permute-start.3
  7.4 3.2 %collective-permute-done.1.message_b = f32[3,64,128]{2,1,0:T(8,128)S(1)} collective-permute-done((f32[3,64,128]{2,1,0:T(8,128)S(1)}, f32[3,64,128]{2,1,0:T(8,128)S(1)}, u32[]{:S(2)}, u32[]{:S(2)}) %collective-permute-start.1) | collective-permute-done | bytes 98336 | tf_op jit(solution)/shard_map/ppermute | solution.py:507
  10.6 0.0 collective-permute-start.4
  10.6 0.2 merge.2.refs_3_
  10.8 0.0 collective-permute-done.3.message_a
  10.8 1.1 %collective-permute-done.4.message_b = f32[3,64,128]{2,1,0:T(8,128)S(1)} collective-permute-done((f32[3,64,128]{2,1,0:T(8,128)S(1)}, f32[3,64,128]{2,1,0:T(8,128)S(1)}, u32[]{:S(2)}, u32[]{:S(2)}) %collective-permute-start.4) | collective-permute-done | bytes 98336 | tf_op jit(solution)/shard_map/ppermute | solution.py:500
  11.9 0.2 merge.3.refs_5_
  12.1 0.0 collective-permute-done.2.refs_4_
  12.1 3.9 %cycles.1 = (f32[2,64,128]{2,1,0:T(8,128)S(1)}, f32[2,64,128]{2,1,0:T(8,128)S(1)}, f32[2,64,128]{2,1,0:T(8,128)S(1)}) custom-call(s32[1,5]{1,0:T(1,128)} %refs_0_.1, f32[1,5]{1,0:T(1,128)} %refs_1_.1, f32[4,2,64,128]{3,2,1,0:T(8,128)S(1)} %get-tuple-element.11.refs_2_, f32[4,2,64,128]{3,2,1,0:T(8,128)S(1)} %merge.2.refs_3_, ...), custom_call_target="tpu_custom_call" | custom-call | tf_op jit(solution)/shard_map/cycles/pallas_call | solution.py:584
  16.0 2.5 %collective-permute-start.7 = (f32[2,64,128]{2,1,0:T(8,128)S(1)}, f32[2,64,128]{2,1,0:T(8,128)S(1)}, u32[]{:S(2)}, u32[]{:S(2)}) collective-permute-start(f32[2,64,128]{2,1,0:T(8,128)S(1)} %get-tuple-element.18), channel_id=1, source_target_pairs={{0,24},{8,16},{16,8},{24,0},{1,25},{9,17},{17,9},{25,1},{2,26},{10... | collective-permute-start | bytes 196616 | tf_op jit(solution)/shard_map/ppermute | solution.py:512
  18.5 0.5 %collective-permute-start.6 = (f32[2,64,128]{2,1,0:T(8,128)S(1)}, f32[2,64,128]{2,1,0:T(8,128)S(1)}, u32[]{:S(2)}, u32[]{:S(2)}) collective-permute-start(f32[2,64,128]{2,1,0:T(8,128)S(1)} %get-tuple-element.18), channel_id=1, source_target_pairs={{0,16},{8,24},{16,0},{24,8},{1,17},{9,25},{17,1},{25,9},{2,18},{10... | collective-permute-start | bytes 196616 | tf_op jit(solution)/shard_map/ppermute | solution.py:512
  19.0 0.5 %collective-permute-start.5 = (f32[2,64,128]{2,1,0:T(8,128)S(1)}, f32[2,64,128]{2,1,0:T(8,128)S(1)}, u32[]{:S(2)}, u32[]{:S(2)}) collective-permute-start(f32[2,64,128]{2,1,0:T(8,128)S(1)} %get-tuple-element.18), channel_id=1, source_target_pairs={{0,8},{8,0},{16,24},{24,16},{1,9},{9,1},{17,25},{25,17},{2,10},{10... | collective-permute-start | bytes 196616 | tf_op jit(solution)/shard_map/ppermute | solution.py:512
  19.6 0.9 %order.1 = (f32[1,2,64,128]{3,2,1,0:T(8,128)}, f32[1,2,64,128]{3,2,1,0:T(8,128)}) custom-call(f32[2,64,128]{2,1,0:T(8,128)S(1)} %get-tuple-element.14.refs_0_, f32[2,64,128]{2,1,0:T(8,128)S(1)} %get-tuple-element.15.refs_1_), custom_call_target="tpu_custom_call" | custom-call | flops 33554432 | bytes 524288 | tf_op jit(solution)/shard_map/order/pallas_call | solution.py:594
  20.4 0.8 %collective-permute-done.7 = f32[2,64,128]{2,1,0:T(8,128)S(1)} collective-permute-done((f32[2,64,128]{2,1,0:T(8,128)S(1)}, f32[2,64,128]{2,1,0:T(8,128)S(1)}, u32[]{:S(2)}, u32[]{:S(2)}) %collective-permute-start.7) | collective-permute-done | bytes 65568 | tf_op jit(solution)/shard_map/ppermute | solution.py:512
  21.3 1.5 %collective-permute-done.6 = f32[2,64,128]{2,1,0:T(8,128)S(1)} collective-permute-done((f32[2,64,128]{2,1,0:T(8,128)S(1)}, f32[2,64,128]{2,1,0:T(8,128)S(1)}, u32[]{:S(2)}, u32[]{:S(2)}) %collective-permute-start.6) | collective-permute-done | bytes 65568 | tf_op jit(solution)/shard_map/ppermute | solution.py:512
  22.8 0.5 %collective-permute-done.5 = f32[2,64,128]{2,1,0:T(8,128)S(1)} collective-permute-done((f32[2,64,128]{2,1,0:T(8,128)S(1)}, f32[2,64,128]{2,1,0:T(8,128)S(1)}, u32[]{:S(2)}, u32[]{:S(2)}) %collective-permute-start.5) | collective-permute-done | bytes 65568 | tf_op jit(solution)/shard_map/ppermute | solution.py:512
  23.3 0.6 %add_add_fusion = f32[2,64,128]{2,1,0:T(8,128)} fusion(f32[2,64,128]{2,1,0:T(8,128)S(1)} %collective-permute-done.6, f32[2,64,128]{2,1,0:T(8,128)S(1)} %collective-permute-done.7, f32[2,64,128]{2,1,0:T(8,128)S(1)} %get-tuple-element.18, f32[2,64,128]{2,1,0:T(8,128)S(1)} %collective-permute-done.5), kind=kLoop, calls=%fused_computation | loop fusion | flops 49152 | bytes 327680 | tf_op jit(solution)/shard_map/add | solution.py:515
Async XLA Ops:
  2.1 10.0 %collective-permute-start.2 = (f32[4,2,64,128]{3,2,1,0:T(8,128)S(1)}, f32[4,2,64,128]{3,2,1,0:T(8,128)S(1)}, u32[]{:S(2)}, u32[]{:S(2)}) collective-permute-start(f32[4,2,64,128]{3,2,1,0:T(8,128)S(1)} %get-tuple-element.11.refs_2_), channel_id=1, source_target_pairs={{4,0},{0,4},{5,1},{1,5},{6,2},{2,6},{7,3},{3,7},{12,8},{8,12},{13,... | collective-permute-start | bytes 786440 | tf_op jit(solution)/shard_map/ppermute | solution.py:500
  2.2 5.2 %collective-permute-start = (f32[3,64,128]{2,1,0:T(8,128)S(1)}, f32[3,64,128]{2,1,0:T(8,128)S(1)}, u32[]{:S(2)}, u32[]{:S(2)}) collective-permute-start(f32[3,64,128]{2,1,0:T(8,128)S(1)} %get-tuple-element.12), channel_id=1, source_target_pairs={{0,1},{1,0},{2,3},{3,2},{4,5},{5,4},{6,7},{7,6},{8,9},{9,8},{10,11... | collective-permute-start | bytes 294920 | tf_op jit(solution)/shard_map/ppermute | solution.py:507
  3.8 6.7 %collective-permute-start.1 = (f32[3,64,128]{2,1,0:T(8,128)S(1)}, f32[3,64,128]{2,1,0:T(8,128)S(1)}, u32[]{:S(2)}, u32[]{:S(2)}) collective-permute-start(f32[3,64,128]{2,1,0:T(8,128)S(1)} %get-tuple-element.13), channel_id=1, source_target_pairs={{1,2},{2,1},{5,6},{6,5},{9,10},{10,9},{13,14},{14,13},{17,18},{18,... | collective-permute-start | bytes 294920 | tf_op jit(solution)/shard_map/ppermute | solution.py:507
  7.4 3.4 %collective-permute-start.3 = (f32[3,64,128]{2,1,0:T(8,128)S(1)}, f32[3,64,128]{2,1,0:T(8,128)S(1)}, u32[]{:S(2)}, u32[]{:S(2)}) collective-permute-start(f32[3,64,128]{2,1,0:T(8,128)S(1)} %collective-permute-done.message_a), channel_id=1, source_target_pairs={{4,0},{0,4},{5,1},{1,5},{6,2},{2,6},{7,3},{3,7},{12,8},{8,12},{13,... | collective-permute-start | bytes 294920 | tf_op jit(solution)/shard_map/ppermute | solution.py:500
  10.6 1.3 %collective-permute-start.4 = (f32[3,64,128]{2,1,0:T(8,128)S(1)}, f32[3,64,128]{2,1,0:T(8,128)S(1)}, u32[]{:S(2)}, u32[]{:S(2)}) collective-permute-start(f32[3,64,128]{2,1,0:T(8,128)S(1)} %collective-permute-done.1.message_b), channel_id=1, source_target_pairs={{4,0},{0,4},{5,1},{1,5},{6,2},{2,6},{7,3},{3,7},{12,8},{8,12},{13,... | collective-permute-start | bytes 294920 | tf_op jit(solution)/shard_map/ppermute | solution.py:500
  16.0 5.3 %collective-permute-start.7 = (f32[2,64,128]{2,1,0:T(8,128)S(1)}, f32[2,64,128]{2,1,0:T(8,128)S(1)}, u32[]{:S(2)}, u32[]{:S(2)}) collective-permute-start(f32[2,64,128]{2,1,0:T(8,128)S(1)} %get-tuple-element.18), channel_id=1, source_target_pairs={{0,24},{8,16},{16,8},{24,0},{1,25},{9,17},{17,9},{25,1},{2,26},{10... | collective-permute-start | bytes 196616 | tf_op jit(solution)/shard_map/ppermute | solution.py:512
  18.5 4.3 %collective-permute-start.6 = (f32[2,64,128]{2,1,0:T(8,128)S(1)}, f32[2,64,128]{2,1,0:T(8,128)S(1)}, u32[]{:S(2)}, u32[]{:S(2)}) collective-permute-start(f32[2,64,128]{2,1,0:T(8,128)S(1)} %get-tuple-element.18), channel_id=1, source_target_pairs={{0,16},{8,24},{16,0},{24,8},{1,17},{9,25},{17,1},{25,9},{2,18},{10... | collective-permute-start | bytes 196616 | tf_op jit(solution)/shard_map/ppermute | solution.py:512
  19.0 4.3 %collective-permute-start.5 = (f32[2,64,128]{2,1,0:T(8,128)S(1)}, f32[2,64,128]{2,1,0:T(8,128)S(1)}, u32[]{:S(2)}, u32[]{:S(2)}) collective-permute-start(f32[2,64,128]{2,1,0:T(8,128)S(1)} %get-tuple-element.18), channel_id=1, source_target_pairs={{0,8},{8,0},{16,24},{24,16},{1,9},{9,1},{17,25},{25,17},{2,10},{10... | collective-permute-start | bytes 196616 | tf_op jit(solution)/shard_map/ppermute | solution.py:512
where the time goes:
time: 24.1 us; the launch traced here: 24 us
  waiting for transfers between devices  8.78 us (36%)
  starting transfers between devices  7.18 us (30%)
  Pallas kernels  6.66 us (28%)
  between operations  0.69 us (3%)
  other arithmetic  0.65 us (3%)
    ppermute x2, waiting for transfers between devices, swapped(): return lax.ppermute(value, axis, pairs)  4.83 us
    pallas_call x1, Pallas kernels, shards(): pl.pallas_call(partial(cycle_kernel, grid_shape, blocks), out_shape=[pltp...  3.91 us
    ppermute x3, starting transfers between devices, summed(): lax.ppermute(value, axis, [(i, i ^ step) for i in range(count)])  3.55 us
    ppermute x2, starting transfers between devices, swapped(): return lax.ppermute(value, axis, pairs)  3.55 us
    ppermute x3, waiting for transfers between devices, summed(): lax.ppermute(value, axis, [(i, i ^ step) for i in range(count)])  2.87 us
    pallas_call x1, Pallas kernels, shards(): pl.pallas_call(pack_kernel, out_shape=[pltpu.VMEM((4,) + block, f32), plt...  1.48 us
    ppermute x3, waiting for transfers between devices, moved(): return lax.ppermute(value, axis, pairs)  1.09 us
    pallas_call x1, Pallas kernels, shards(): pl.pallas_call(order_kernel, out_shape=[state] * 2, in_specs=[vmem] * 2,...  0.86 us
  transfers between devices with their start and end apart: 8, of which 6 were waited for; matrix products, arithmetic and copies ran while one was open for 0% of the time, Pallas kernels for 5%

commit v1 on v0

--- a/solution.py
+++ b/solution.py
@@ -80,7 +80,7 @@
             ordered[layer, pl.ds(t, SUB, stride=count), :] = natural[layer, t * SUB:(t + 1) * SUB]
 
 
-def pack_kernel(scale_hbm, perm_log_hbm, facies_hbm, acc_hbm, prev_hbm, obs_hbm, own, message_a, message_b,
+def pack_kernel(scale_hbm, perm_log_hbm, facies_hbm, acc_hbm, prev_hbm, obs_hbm, own_a, own_b, message_a, message_b,
                 scale, perm_log, facies, acc, prev, obs, sems):
     pairs = ((scale_hbm, scale), (perm_log_hbm, perm_log), (facies_hbm, facies), (acc_hbm, acc), (prev_hbm, prev),
              (obs_hbm, obs))
@@ -99,7 +99,7 @@
         factor = factor + jnp.where(label == number, scale[number], jnp.float32(0.0))
     fields = [shuffle(value, False) for value in (jnp.exp(layers(perm_log)) * factor, layers(acc), layers(prev.at[0]), layers(obs.at[0]))]
     for number in range(4):
-        own[number] = fields[number]
+        (own_a, own_b)[number // 2][number % 2] = fields[number]
     place = place_in_half(label.shape)
     full = []
     for number in range(3):
@@ -393,8 +393,8 @@
 
 def cycle_kernel(grid_shape, blocks, *refs):
     cells_hbm, rates_hbm = refs[:2]
-    inputs = [refs[2 + 2 * b:4 + 2 * b] for b in range(blocks)]
-    refs = refs[2 + 2 * blocks:]
+    inputs = [refs[2 + 3 * b:5 + 3 * b] for b in range(blocks)]
+    refs = refs[2 + 3 * blocks:]
     pressure_out, adjoint_out, terms_out = refs[:3]
     cells, rates, sems, perm, acc, middle_acc, bottom_acc, states, terms_rows = refs[3:12]
     refs = refs[12:]
@@ -411,7 +411,8 @@
 
     def fields(number, layer, b, t):
         low = lane_index() < HALF
-        own, beside = [value[number, layer, rows(t), :] for value in inputs[b]]
+        own = inputs[b][number // 2][number % 2, layer, rows(t), :]
+        beside = inputs[b][2][number, layer, rows(t), :]
         return jnp.where(low, own, beside), lane_roll(jnp.where(low, beside, own), HALF)
 
     gx = lax.axis_index("gx")
@@ -541,15 +542,16 @@
     f32 = jnp.float32
     fields = (perm_log, facies, accumulation, previous_pressure, observed)
     block = (layer_count, row_count, col_count)
-    own, message_a, message_b = pl.pallas_call(
+    own_a, own_b, message_a, message_b = pl.pallas_call(
         pack_kernel,
         out_shape=[
-            pltpu.VMEM((4,) + block, f32),
+            pltpu.VMEM((2,) + block, f32),
+            pltpu.VMEM((2,) + block, f32),
             pltpu.VMEM((3,) + block[1:], f32),
             pltpu.VMEM((3,) + block[1:], f32),
         ],
         in_specs=[hbm] * 6,
-        out_specs=[vmem] * 3,
+        out_specs=[vmem] * 4,
         scratch_shapes=[pltpu.SMEM(facies_scale.shape, f32)]
         + [pltpu.VMEM(value.shape, value.dtype) for value in fields] + [pltpu.SemaphoreType.DMA((6,))],
         name="pack",
@@ -557,7 +559,7 @@
 
     steps = (0, 1) if gx_count == 2 else (0, 1, -1) if gx_count > 2 else (0,)
     blocks = len(steps)
-    owns = [own] + [moved(own, "gx", step) for step in steps[1:]]
+    owns = [(own_a, own_b)] + [(moved(own_a, "gx", step), moved(own_b, "gx", step)) for step in steps[1:]]
     merge = pl.pallas_call(
         merge_kernel,
         out_shape=pltpu.VMEM((4,) + block, f32),
@@ -570,7 +572,7 @@
     besides = [merge(*[in_vmem(value) for value in messages])]
     for step in steps[1:]:
         besides.append(merge(*[in_vmem(moved(value, "gx", step)) for value in messages]))
-    operands = [in_vmem(value) for pair in zip(owns, besides) for value in pair]
+    operands = [in_vmem(value) for own, beside in zip(owns, besides) for value in (*own, beside)]
 
     count = row_count // SUB
     scratch = [pltpu.SMEM(well_cells.shape, jnp.int32), pltpu.SMEM(well_rates.shape, f32), pltpu.SemaphoreType.DMA((2,))]
@@ -584,7 +586,7 @@
     *shuffled, terms = pl.pallas_call(
         partial(cycle_kernel, grid_shape, blocks),
         out_shape=[pltpu.VMEM(block, f32)] * 3,
-        in_specs=[hbm] * 2 + [vmem] * (2 * blocks),
+        in_specs=[hbm] * 2 + [vmem] * (3 * blocks),
         out_specs=[vmem] * 3,
         scratch_shapes=scratch,
         compiler_params=pltpu.CompilerParams(vmem_limit_bytes=24 * 1024 * 1024),

time: 24.1 us -> 23.8 us (0.988)
  waiting for transfers between devices: 8.78 us -> 7.96 us
  starting transfers between devices: 7.18 us -> 7.68 us
    ppermute x2, waiting for transfers between devices: 4.83 us -> 4 us  [swapped(): return lax.ppermute(value, axis, pairs)]
    ppermute x3 -> x4, starting transfers between devices: 0.08 us -> 0.57 us  [moved(): return lax.ppermute(value, axis, pairs)]
    ppermute x3 -> x4, waiting for transfers between devices: 1.09 us -> 1.09 us  [moved(): return lax.ppermute(value, axis, pairs)]
  transfers between devices with their start and end apart: 8 -> 9, of which waited for: 6 -> 6; matrix products, arithmetic and copies ran while one was open for 0% -> 0% of each run, Pallas kernels for 5% -> 5%
where the time goes in v1:
time: 23.8 us; the launch traced here: 23.6 us
  waiting for transfers between devices  7.96 us (33%)
  starting transfers between devices  7.68 us (32%)
  Pallas kernels  6.65 us (28%)
  between operations  0.7 us (3%)
  other arithmetic  0.65 us (3%)
    ppermute x2, waiting for transfers between devices, swapped(): return lax.ppermute(value, axis, pairs)  4 us
    pallas_call x1, Pallas kernels, shards(): pl.pallas_call(partial(cycle_kernel, grid_shape, blocks), out_shape=[pltp...  3.91 us
    ppermute x3, starting transfers between devices, summed(): lax.ppermute(value, axis, [(i, i ^ step) for i in range(count)])  3.55 us
    ppermute x2, starting transfers between devices, swapped(): return lax.ppermute(value, axis, pairs)  3.55 us
    ppermute x3, waiting for transfers between devices, summed(): lax.ppermute(value, axis, [(i, i ^ step) for i in range(count)])  2.86 us
    pallas_call x1, Pallas kernels, shards(): pl.pallas_call(pack_kernel, out_shape=[pltpu.VMEM((2,) + block, f32), plt...  1.48 us
    ppermute x4, waiting for transfers between devices, moved(): return lax.ppermute(value, axis, pairs)  1.09 us
    pallas_call x1, Pallas kernels, shards(): pl.pallas_call(order_kernel, out_shape=[state] * 2, in_specs=[vmem] * 2,...  0.86 us
  transfers between devices with their start and end apart: 9, of which 6 were waited for; matrix products, arithmetic and copies ran while one was open for 0% of the time, Pallas kernels for 5%

profile of v1, /device:TPU:16, one launch (start us, length us, event | category | flops | bytes accessed | tf_op | source)
XLA Modules:
  0.0 23.6 jit_solution(2314248827346033760)
XLA Ops:
  0.6 1.5 %pack.1 = (f32[2,2,64,128]{3,2,1,0:T(8,128)S(1)}, f32[2,2,64,128]{3,2,1,0:T(8,128)S(1)}, f32[3,64,128]{2,1,0:T(8,128)S(1)}, f32[3,64,128]{2,1,0:T(8,128)S(1)}) custom-call(f32[4]{0:T(128)} %scale_hbm.1, f32[2,64,128]{2,1,0:T(8,128)} %perm_log_hbm.1, s32[2,64,128]{2,1,0:T(8,128)} %facies_hbm.1, f32[2,64,128]{2,1,0:T(8,128)} %acc_hbm.1, ...), custom_call_target="tpu_custom_call" | custom-call | tf_op jit(solution)/shard_map/pack/pallas_call | solution.py:545
  2.1 1.6 %collective-permute-start = (f32[3,64,128]{2,1,0:T(8,128)S(1)}, f32[3,64,128]{2,1,0:T(8,128)S(1)}, u32[]{:S(2)}, u32[]{:S(2)}) collective-permute-start(f32[3,64,128]{2,1,0:T(8,128)S(1)} %get-tuple-element.14), channel_id=1, source_target_pairs={{0,1},{1,0},{2,3},{3,2},{4,5},{5,4},{6,7},{7,6},{8,9},{9,8},{10,11... | collective-permute-start | bytes 294920 | tf_op jit(solution)/shard_map/ppermute | solution.py:508
  3.8 1.9 %collective-permute-start.1 = (f32[3,64,128]{2,1,0:T(8,128)S(1)}, f32[3,64,128]{2,1,0:T(8,128)S(1)}, u32[]{:S(2)}, u32[]{:S(2)}) collective-permute-start(f32[3,64,128]{2,1,0:T(8,128)S(1)} %get-tuple-element.15), channel_id=1, source_target_pairs={{1,2},{2,1},{5,6},{6,5},{9,10},{10,9},{13,14},{14,13},{17,18},{18,... | collective-permute-start | bytes 294920 | tf_op jit(solution)/shard_map/ppermute | solution.py:508
  5.7 0.1 collective-permute-start.2
  5.8 0.5 %collective-permute-start.3 = (f32[2,2,64,128]{3,2,1,0:T(8,128)S(1)}, f32[2,2,64,128]{3,2,1,0:T(8,128)S(1)}, u32[]{:S(2)}, u32[]{:S(2)}) collective-permute-start(f32[2,2,64,128]{3,2,1,0:T(8,128)S(1)} %get-tuple-element.13.refs_3_), channel_id=1, source_target_pairs={{4,0},{0,4},{5,1},{1,5},{6,2},{2,6},{7,3},{3,7},{12,8},{8,12},{13,... | collective-permute-start | bytes 393224 | tf_op jit(solution)/shard_map/ppermute | solution.py:501
  6.3 0.5 %collective-permute-done.message_a = f32[3,64,128]{2,1,0:T(8,128)S(1)} collective-permute-done((f32[3,64,128]{2,1,0:T(8,128)S(1)}, f32[3,64,128]{2,1,0:T(8,128)S(1)}, u32[]{:S(2)}, u32[]{:S(2)}) %collective-permute-start) | collective-permute-done | bytes 98336 | tf_op jit(solution)/shard_map/ppermute | solution.py:508
  6.8 0.0 collective-permute-start.4
  6.8 3.5 %collective-permute-done.1.message_b = f32[3,64,128]{2,1,0:T(8,128)S(1)} collective-permute-done((f32[3,64,128]{2,1,0:T(8,128)S(1)}, f32[3,64,128]{2,1,0:T(8,128)S(1)}, u32[]{:S(2)}, u32[]{:S(2)}) %collective-permute-start.1) | collective-permute-done | bytes 98336 | tf_op jit(solution)/shard_map/ppermute | solution.py:508
  10.3 0.0 collective-permute-start.5
  10.3 0.2 merge.2.refs_4_
  10.5 0.0 collective-permute-done.4.message_a
  10.5 1.1 %collective-permute-done.5.message_b = f32[3,64,128]{2,1,0:T(8,128)S(1)} collective-permute-done((f32[3,64,128]{2,1,0:T(8,128)S(1)}, f32[3,64,128]{2,1,0:T(8,128)S(1)}, u32[]{:S(2)}, u32[]{:S(2)}) %collective-permute-start.5) | collective-permute-done | bytes 98336 | tf_op jit(solution)/shard_map/ppermute | solution.py:501
  11.6 0.2 merge.3.refs_7_
  11.8 0.0 collective-permute-done.2.refs_5_
  11.8 0.0 collective-permute-done.3.refs_6_
  11.8 3.9 %cycles.1 = (f32[2,64,128]{2,1,0:T(8,128)S(1)}, f32[2,64,128]{2,1,0:T(8,128)S(1)}, f32[2,64,128]{2,1,0:T(8,128)S(1)}) custom-call(s32[1,5]{1,0:T(1,128)} %refs_0_.1, f32[1,5]{1,0:T(1,128)} %refs_1_.1, f32[2,2,64,128]{3,2,1,0:T(8,128)S(1)} %get-tuple-element.12.refs_2_, f32[2,2,64,128]{3,2,1,0:T(8,128)S(1)} %get-tuple-element.13.refs_3_, ...), custom_call_target="tpu_custom_call" | custom-call | tf_op jit(solution)/shard_map/cycles/pallas_call | solution.py:586
  15.7 2.5 %collective-permute-start.8 = (f32[2,64,128]{2,1,0:T(8,128)S(1)}, f32[2,64,128]{2,1,0:T(8,128)S(1)}, u32[]{:S(2)}, u32[]{:S(2)}) collective-permute-start(f32[2,64,128]{2,1,0:T(8,128)S(1)} %get-tuple-element.20), channel_id=1, source_target_pairs={{0,24},{8,16},{16,8},{24,0},{1,25},{9,17},{17,9},{25,1},{2,26},{10... | collective-permute-start | bytes 196616 | tf_op jit(solution)/shard_map/ppermute | solution.py:513
  18.2 0.5 %collective-permute-start.7 = (f32[2,64,128]{2,1,0:T(8,128)S(1)}, f32[2,64,128]{2,1,0:T(8,128)S(1)}, u32[]{:S(2)}, u32[]{:S(2)}) collective-permute-start(f32[2,64,128]{2,1,0:T(8,128)S(1)} %get-tuple-element.20), channel_id=1, source_target_pairs={{0,16},{8,24},{16,0},{24,8},{1,17},{9,25},{17,1},{25,9},{2,18},{10... | collective-permute-start | bytes 196616 | tf_op jit(solution)/shard_map/ppermute | solution.py:513
  18.7 0.5 %collective-permute-start.6 = (f32[2,64,128]{2,1,0:T(8,128)S(1)}, f32[2,64,128]{2,1,0:T(8,128)S(1)}, u32[]{:S(2)}, u32[]{:S(2)}) collective-permute-start(f32[2,64,128]{2,1,0:T(8,128)S(1)} %get-tuple-element.20), channel_id=1, source_target_pairs={{0,8},{8,0},{16,24},{24,16},{1,9},{9,1},{17,25},{25,17},{2,10},{10... | collective-permute-start | bytes 196616 | tf_op jit(solution)/shard_map/ppermute | solution.py:513
  19.3 0.9 %order.1 = (f32[1,2,64,128]{3,2,1,0:T(8,128)}, f32[1,2,64,128]{3,2,1,0:T(8,128)}) custom-call(f32[2,64,128]{2,1,0:T(8,128)S(1)} %get-tuple-element.16.refs_0_, f32[2,64,128]{2,1,0:T(8,128)S(1)} %get-tuple-element.17.refs_1_), custom_call_target="tpu_custom_call" | custom-call | flops 33554432 | bytes 524288 | tf_op jit(solution)/shard_map/order/pallas_call | solution.py:596
  20.1 0.8 %collective-permute-done.8 = f32[2,64,128]{2,1,0:T(8,128)S(1)} collective-permute-done((f32[2,64,128]{2,1,0:T(8,128)S(1)}, f32[2,64,128]{2,1,0:T(8,128)S(1)}, u32[]{:S(2)}, u32[]{:S(2)}) %collective-permute-start.8) | collective-permute-done | bytes 65568 | tf_op jit(solution)/shard_map/ppermute | solution.py:513
  21.0 1.5 %collective-permute-done.7 = f32[2,64,128]{2,1,0:T(8,128)S(1)} collective-permute-done((f32[2,64,128]{2,1,0:T(8,128)S(1)}, f32[2,64,128]{2,1,0:T(8,128)S(1)}, u32[]{:S(2)}, u32[]{:S(2)}) %collective-permute-start.7) | collective-permute-done | bytes 65568 | tf_op jit(solution)/shard_map/ppermute | solution.py:513
  22.5 0.5 %collective-permute-done.6 = f32[2,64,128]{2,1,0:T(8,128)S(1)} collective-permute-done((f32[2,64,128]{2,1,0:T(8,128)S(1)}, f32[2,64,128]{2,1,0:T(8,128)S(1)}, u32[]{:S(2)}, u32[]{:S(2)}) %collective-permute-start.6) | collective-permute-done | bytes 65568 | tf_op jit(solution)/shard_map/ppermute | solution.py:513
  23.0 0.6 %add_add_fusion = f32[2,64,128]{2,1,0:T(8,128)} fusion(f32[2,64,128]{2,1,0:T(8,128)S(1)} %collective-permute-done.7, f32[2,64,128]{2,1,0:T(8,128)S(1)} %collective-permute-done.8, f32[2,64,128]{2,1,0:T(8,128)S(1)} %get-tuple-element.20, f32[2,64,128]{2,1,0:T(8,128)S(1)} %collective-permute-done.6), kind=kLoop, calls=%fused_computation | loop fusion | flops 49152 | bytes 327680 | tf_op jit(solution)/shard_map/add | solution.py:516
Async XLA Ops:
  2.1 4.7 %collective-permute-start = (f32[3,64,128]{2,1,0:T(8,128)S(1)}, f32[3,64,128]{2,1,0:T(8,128)S(1)}, u32[]{:S(2)}, u32[]{:S(2)}) collective-permute-start(f32[3,64,128]{2,1,0:T(8,128)S(1)} %get-tuple-element.14), channel_id=1, source_target_pairs={{0,1},{1,0},{2,3},{3,2},{4,5},{5,4},{6,7},{7,6},{8,9},{9,8},{10,11... | collective-permute-start | bytes 294920 | tf_op jit(solution)/shard_map/ppermute | solution.py:508
  3.8 6.5 %collective-permute-start.1 = (f32[3,64,128]{2,1,0:T(8,128)S(1)}, f32[3,64,128]{2,1,0:T(8,128)S(1)}, u32[]{:S(2)}, u32[]{:S(2)}) collective-permute-start(f32[3,64,128]{2,1,0:T(8,128)S(1)} %get-tuple-element.15), channel_id=1, source_target_pairs={{1,2},{2,1},{5,6},{6,5},{9,10},{10,9},{13,14},{14,13},{17,18},{18,... | collective-permute-start | bytes 294920 | tf_op jit(solution)/shard_map/ppermute | solution.py:508
  5.7 6.1 %collective-permute-start.2 = (f32[2,2,64,128]{3,2,1,0:T(8,128)S(1)}, f32[2,2,64,128]{3,2,1,0:T(8,128)S(1)}, u32[]{:S(2)}, u32[]{:S(2)}) collective-permute-start(f32[2,2,64,128]{3,2,1,0:T(8,128)S(1)} %get-tuple-element.12.refs_2_), channel_id=1, source_target_pairs={{4,0},{0,4},{5,1},{1,5},{6,2},{2,6},{7,3},{3,7},{12,8},{8,12},{13,... | collective-permute-start | bytes 393224 | tf_op jit(solution)/shard_map/ppermute | solution.py:501
  5.8 6.0 %collective-permute-start.3 = (f32[2,2,64,128]{3,2,1,0:T(8,128)S(1)}, f32[2,2,64,128]{3,2,1,0:T(8,128)S(1)}, u32[]{:S(2)}, u32[]{:S(2)}) collective-permute-start(f32[2,2,64,128]{3,2,1,0:T(8,128)S(1)} %get-tuple-element.13.refs_3_), channel_id=1, source_target_pairs={{4,0},{0,4},{5,1},{1,5},{6,2},{2,6},{7,3},{3,7},{12,8},{8,12},{13,... | collective-permute-start | bytes 393224 | tf_op jit(solution)/shard_map/ppermute | solution.py:501
  6.8 3.7 %collective-permute-start.4 = (f32[3,64,128]{2,1,0:T(8,128)S(1)}, f32[3,64,128]{2,1,0:T(8,128)S(1)}, u32[]{:S(2)}, u32[]{:S(2)}) collective-permute-start(f32[3,64,128]{2,1,0:T(8,128)S(1)} %collective-permute-done.message_a), channel_id=1, source_target_pairs={{4,0},{0,4},{5,1},{1,5},{6,2},{2,6},{7,3},{3,7},{12,8},{8,12},{13,... | collective-permute-start | bytes 294920 | tf_op jit(solution)/shard_map/ppermute | solution.py:501
  10.3 1.3 %collective-permute-start.5 = (f32[3,64,128]{2,1,0:T(8,128)S(1)}, f32[3,64,128]{2,1,0:T(8,128)S(1)}, u32[]{:S(2)}, u32[]{:S(2)}) collective-permute-start(f32[3,64,128]{2,1,0:T(8,128)S(1)} %collective-permute-done.1.message_b), channel_id=1, source_target_pairs={{4,0},{0,4},{5,1},{1,5},{6,2},{2,6},{7,3},{3,7},{12,8},{8,12},{13,... | collective-permute-start | bytes 294920 | tf_op jit(solution)/shard_map/ppermute | solution.py:501
  15.7 5.3 %collective-permute-start.8 = (f32[2,64,128]{2,1,0:T(8,128)S(1)}, f32[2,64,128]{2,1,0:T(8,128)S(1)}, u32[]{:S(2)}, u32[]{:S(2)}) collective-permute-start(f32[2,64,128]{2,1,0:T(8,128)S(1)} %get-tuple-element.20), channel_id=1, source_target_pairs={{0,24},{8,16},{16,8},{24,0},{1,25},{9,17},{17,9},{25,1},{2,26},{10... | collective-permute-start | bytes 196616 | tf_op jit(solution)/shard_map/ppermute | solution.py:513
  18.2 4.3 %collective-permute-start.7 = (f32[2,64,128]{2,1,0:T(8,128)S(1)}, f32[2,64,128]{2,1,0:T(8,128)S(1)}, u32[]{:S(2)}, u32[]{:S(2)}) collective-permute-start(f32[2,64,128]{2,1,0:T(8,128)S(1)} %get-tuple-element.20), channel_id=1, source_target_pairs={{0,16},{8,24},{16,0},{24,8},{1,17},{9,25},{17,1},{25,9},{2,18},{10... | collective-permute-start | bytes 196616 | tf_op jit(solution)/shard_map/ppermute | solution.py:513
  18.7 4.3 %collective-permute-start.6 = (f32[2,64,128]{2,1,0:T(8,128)S(1)}, f32[2,64,128]{2,1,0:T(8,128)S(1)}, u32[]{:S(2)}, u32[]{:S(2)}) collective-permute-start(f32[2,64,128]{2,1,0:T(8,128)S(1)} %get-tuple-element.20), channel_id=1, source_target_pairs={{0,8},{8,0},{16,24},{24,16},{1,9},{9,1},{17,25},{25,17},{2,10},{10... | collective-permute-start | bytes 196616 | tf_op jit(solution)/shard_map/ppermute | solution.py:513

commit v2 on v1

--- a/solution.py
+++ b/solution.py
@@ -116,7 +116,7 @@
         message_b[plane] = jnp.where(left_first, second, first)
 
 
-def merge_kernel(message_a, message_b, beside):
+def merge(message_a, message_b, beside):
     place = place_in_half(beside.shape[2:])
     from_a = (place < HALF // 2) != (lax.axis_index("gy") % 2 == 1)
     full = [[], [], []]
@@ -137,6 +137,47 @@
         beside[OBS, layer] = observed
 
 
+def block_kernel(own_a, own_b, message_a, message_b, vectors, c_south, c_inner, c_east, c_west, c_layer, beside):
+    merge(message_a, message_b, beside)
+    count = own_a.shape[2] // SUB
+    low = lane_index() < HALF
+    perm = {}
+    for t in range(count):
+        rows = pl.ds(t * SUB, SUB)
+        for layer in range(LAYERS):
+            for number in range(4):
+                own, outer = (own_a, own_b)[number // 2][number % 2, layer, rows, :], beside[number, layer, rows, :]
+                pair = jnp.where(low, own, outer), lane_roll(jnp.where(low, outer, own), HALF)
+                for u in range(2):
+                    vectors[number, layer, u, t] = pair[u]
+                    if number == PERM:
+                        perm[layer, u, t] = pair[u]
+            even, odd = perm[layer, 0, t], perm[layer, 1, t]
+            c_inner[layer, t] = harmonic(even, odd)
+            east = harmonic(odd, lane_roll(even, -1))
+            c_east[layer, t] = east
+            c_west[layer, t] = lane_roll(east, 1)
+            for u in range(2):
+                if t > 0:
+                    c_south[layer, u, t - 1] = harmonic(perm[layer, u, t - 1], perm[layer, u, t])
+        for u in range(2):
+            c_layer[u, t] = vertical * harmonic(perm[0, u, t], perm[1, u, t])
+
+
+class Blocks:
+    def __init__(self, refs, field=None, last=None):
+        self.refs = refs
+        self.field = () if field is None else (field,)
+        self.last = last
+
+    def __getitem__(self, key):
+        *lead, b, t = key
+        ref = self.refs[b]
+        if self.last is not None and t == ref.shape[-3] - 1:
+            return self.last[(*lead, b)]
+        return ref[(*self.field, *lead, t)]
+
+
 class Level:
     def __init__(self, count, width, span, blocks, refs):
         self.count = count
@@ -150,6 +191,9 @@
     def scratch(count, width, blocks):
         def vectors(*lead):
             return pltpu.VMEM(lead + (SUB, LANES), jnp.float32)
+
+        if width == 2:
+            return [vectors(LAYERS, width, blocks)] * 2 + [vectors(LAYERS, width, blocks, count)] * 5
 
         whole = vectors(LAYERS, width, blocks, count)
         edge = vectors(LAYERS, blocks, count)
@@ -298,29 +342,19 @@
     return 2.0 * left * right / jnp.maximum(left + right, 1e-20)
 
 
-def finest_coeffs(level, perm, joined):
+def joining_coeffs(level, perm, c_last, joined):
     last = level.count - 1
+    edge = row_index() >= SUB - 1
     for layer, u in level.members():
-        heads = [perm[layer, u, b, 0] for b in range(level.blocks)]
-        rolled = [row_roll(value, -1) for value in heads]
-        edge = row_index() >= SUB - 1
+        rolled = [row_roll(perm[layer, u, b, 0], -1) for b in range(level.blocks)]
+        souths = []
         for b in range(level.blocks):
             after = jnp.where(edge, joined[b] * rolled[(b + 1) % level.blocks], rolled[b])
-            for t in range(level.count):
-                beyond = perm[layer, u, b, t + 1] if t < last else after
-                level.c_south[layer, u, b, t] = harmonic(perm[layer, u, b, t], beyond)
-        firsts = row_before([level.c_south[layer, u, b, last] for b in range(level.blocks)])
+            souths.append(harmonic(perm[layer, u, b, last], after))
+        firsts = row_before(souths)
         for b in range(level.blocks):
+            c_last[layer, u, b] = souths[b]
             level.c_first[layer, u, b] = firsts[b]
-    for b, t in level.steps():
-        for u in range(level.width):
-            level.c_layer[u, b, t] = vertical * harmonic(perm[0, u, b, t], perm[1, u, b, t])
-        for layer in range(LAYERS):
-            even, odd = perm[layer, 0, b, t], perm[layer, 1, b, t]
-            level.c_inner[layer, b, t] = harmonic(even, odd)
-            east = harmonic(odd, lane_roll(even, -1))
-            level.c_east[layer, b, t] = east
-            level.c_west[layer, b, t] = lane_roll(east, 1)
 
 
 def with_weight(level, acc):
@@ -393,27 +427,25 @@
 
 def cycle_kernel(grid_shape, blocks, *refs):
     cells_hbm, rates_hbm = refs[:2]
-    inputs = [refs[2 + 3 * b:5 + 3 * b] for b in range(blocks)]
-    refs = refs[2 + 3 * blocks:]
+    inputs = list(zip(*[refs[2 + 6 * b:8 + 6 * b] for b in range(blocks)]))
+    refs = refs[2 + 6 * blocks:]
     pressure_out, adjoint_out, terms_out = refs[:3]
-    cells, rates, sems, perm, acc, middle_acc, bottom_acc, states, terms_rows = refs[3:12]
-    refs = refs[12:]
+    cells, rates, sems, middle_acc, bottom_acc, states, terms_rows = refs[3:10]
+    refs = refs[10:]
     copies = [pltpu.make_async_copy(cells_hbm, cells, sems.at[0]), pltpu.make_async_copy(rates_hbm, rates, sems.at[1])]
     for copy in copies:
         copy.start()
-    count = inputs[0][0].shape[2] // SUB
-    levels = [Level(count >> depth, width, span, blocks, refs[11 * depth:11 * depth + 11])
+    perm, acc, previous, observed = [Blocks(inputs[0], number) for number in range(4)]
+    count = inputs[0][0].shape[3]
+    c_last = refs[0]
+    coeffs = [Blocks(inputs[1], last=c_last), refs[1]] + [Blocks(value) for value in inputs[2:]]
+    level_refs = [coeffs + list(refs[2:7]), refs[7:18], refs[18:29]]
+    levels = [Level(count >> depth, width, span, blocks, level_refs[depth])
               for depth, (width, span) in enumerate(LEVELS)]
     finest, middle, bottom = levels
 
     def rows(t):
         return pl.ds(t * SUB, SUB)
-
-    def fields(number, layer, b, t):
-        low = lane_index() < HALF
-        own = inputs[b][number // 2][number % 2, layer, rows(t), :]
-        beside = inputs[b][2][number, layer, rows(t), :]
-        return jnp.where(low, own, beside), lane_roll(jnp.where(low, beside, own), HALF)
 
     gx = lax.axis_index("gx")
     if blocks == 3:
@@ -424,14 +456,11 @@
         joined = [0.0]
 
     for b, t in finest.steps():
-        for layer in range(LAYERS):
-            perms, accs, starts = [fields(number, layer, b, t) for number in (PERM, ACC, PREV)]
-            for u in range(2):
-                key = layer, u, b, t
-                perm[key] = perms[u]
-                acc[key] = accs[u]
-                finest.now[key] = starts[u]
-                finest.target[key] = accs[u] * starts[u]
+        for layer, u in finest.members():
+            key = layer, u, b, t
+            start = previous[key]
+            finest.now[key] = start
+            finest.target[key] = acc[key] * start
 
     for copy in copies:
         copy.wait()
@@ -459,7 +488,7 @@
         hit = (row_index() == in_block // count) & (lane_index() == col // 2)
         finest.target[place] = finest.target[place] + jnp.where(hit, rate, 0.0)
 
-    finest_coeffs(finest, perm, joined)
+    joining_coeffs(finest, perm, c_last, joined)
     with_weight(finest, acc)
     coarse_coeffs(finest, middle, acc, middle_acc)
     coarse_coeffs(middle, bottom, middle_acc, bottom_acc)
@@ -471,15 +500,13 @@
         finest.now, finest.later = start, other
         vcycle(levels)
         for b, t in finest.steps():
-            for layer in range(LAYERS):
-                observed = fields(OBS, layer, b, t)
-                for u in range(2):
-                    key = layer, u, b, t
-                    value = finest.now[key]
-                    states[(number,) + key] = value
-                    target = value - observed[u]
-                    finest.target[key] = target
-                    start[key] = finest.weight[key] * target
+            for layer, u in finest.members():
+                key = layer, u, b, t
+                value = finest.now[key]
+                states[(number,) + key] = value
+                target = value - observed[key]
+                finest.target[key] = target
+                start[key] = finest.weight[key] * target
         return carry
 
     lax.fori_loop(0, 2, turn, 0)
@@ -560,24 +587,30 @@
     steps = (0, 1) if gx_count == 2 else (0, 1, -1) if gx_count > 2 else (0,)
     blocks = len(steps)
     owns = [(own_a, own_b)] + [(moved(own_a, "gx", step), moved(own_b, "gx", step)) for step in steps[1:]]
-    merge = pl.pallas_call(
-        merge_kernel,
-        out_shape=pltpu.VMEM((4,) + block, f32),
-        in_specs=[vmem] * 2,
-        out_specs=vmem,
-        cost_estimate=pl.CostEstimate(flops=2**20, bytes_accessed=2**19, transcendentals=0),
-        name="merge",
+    count = row_count // SUB
+
+    def vectors(*lead):
+        return pltpu.VMEM(lead + (count, SUB, LANES), f32)
+
+    level_zero = pl.pallas_call(
+        block_kernel,
+        out_shape=[vectors(4, LAYERS, 2), vectors(LAYERS, 2)] + [vectors(LAYERS)] * 3 + [vectors(2)],
+        in_specs=[vmem] * 4,
+        out_specs=[vmem] * 6,
+        scratch_shapes=[pltpu.VMEM((4,) + block, f32)],
+        cost_estimate=pl.CostEstimate(flops=2**21, bytes_accessed=2**21, transcendentals=0),
+        name="level_zero",
     )
     messages = swapped(message_a, "gy", 0), swapped(message_b, "gy", 1)
-    besides = [merge(*[in_vmem(value) for value in messages])]
-    for step in steps[1:]:
-        besides.append(merge(*[in_vmem(moved(value, "gx", step)) for value in messages]))
-    operands = [in_vmem(value) for own, beside in zip(owns, besides) for value in (*own, beside)]
-
-    count = row_count // SUB
+    operands = []
+    for (one, two), step in zip(owns, steps):
+        sides = messages if step == 0 else [moved(value, "gx", step) for value in messages]
+        operands += level_zero(*[in_vmem(value) for value in (one, two, *sides)])
+    operands = [in_vmem(value) for value in operands]
+
     scratch = [pltpu.SMEM(well_cells.shape, jnp.int32), pltpu.SMEM(well_rates.shape, f32), pltpu.SemaphoreType.DMA((2,))]
     whole = [pltpu.VMEM((LAYERS, width, blocks, count >> depth, SUB, LANES), f32) for depth, (width, _) in enumerate(LEVELS)]
-    scratch += [whole[0], whole[0], whole[1], whole[2]]
+    scratch += [whole[1], whole[2]]
     scratch += [pltpu.VMEM((2, LAYERS, 2, blocks, count, SUB, LANES), f32), pltpu.VMEM(block, f32)]
     for depth, (width, _) in enumerate(LEVELS):
         scratch += Level.scratch(count >> depth, width, blocks)
@@ -586,7 +619,7 @@
     *shuffled, terms = pl.pallas_call(
         partial(cycle_kernel, grid_shape, blocks),
         out_shape=[pltpu.VMEM(block, f32)] * 3,
-        in_specs=[hbm] * 2 + [vmem] * (3 * blocks),
+        in_specs=[hbm] * 2 + [vmem] * (6 * blocks),
         out_specs=[vmem] * 3,
         scratch_shapes=scratch,
         compiler_params=pltpu.CompilerParams(vmem_limit_bytes=24 * 1024 * 1024),

time: 23.8 us -> 23.9 us (level)
  Pallas kernels: 6.65 us -> 6.95 us
  waiting for transfers between devices: 7.96 us -> 7.72 us
    pallas_call x2, Pallas kernels: 0.4 us -> 0.83 us  [shards(): operands += level_zero(*[in_vmem(value) for value in (one, two, *sides)])]
    ppermute x4, waiting for transfers between devices: 1.09 us -> 0.85 us  [moved(): return lax.ppermute(value, axis, pairs)]
where the time goes in v2:
time: 23.9 us; the launch traced here: 23.7 us
  waiting for transfers between devices  7.72 us (32%)
  starting transfers between devices  7.68 us (32%)
  Pallas kernels  6.95 us (29%)
  between operations  0.71 us (3%)
  other arithmetic  0.65 us (3%)
    ppermute x2, waiting for transfers between devices, swapped(): return lax.ppermute(value, axis, pairs)  4 us
    pallas_call x1, Pallas kernels, shards(): pl.pallas_call(partial(cycle_kernel, grid_shape, blocks), out_shape=[pltp...  3.78 us
    ppermute x3, starting transfers between devices, summed(): lax.ppermute(value, axis, [(i, i ^ step) for i in range(count)])  3.55 us
    ppermute x2, starting transfers between devices, swapped(): return lax.ppermute(value, axis, pairs)  3.55 us
    ppermute x3, waiting for transfers between devices, summed(): lax.ppermute(value, axis, [(i, i ^ step) for i in range(count)])  2.87 us
    pallas_call x1, Pallas kernels, shards(): pl.pallas_call(pack_kernel, out_shape=[pltpu.VMEM((2,) + block, f32), plt...  1.48 us
    pallas_call x1, Pallas kernels, shards(): pl.pallas_call(order_kernel, out_shape=[state] * 2, in_specs=[vmem] * 2,...  0.86 us
    ppermute x4, waiting for transfers between devices, moved(): return lax.ppermute(value, axis, pairs)  0.85 us
  transfers between devices with their start and end apart: 9, of which 6 were waited for; matrix products, arithmetic and copies ran while one was open for 0% of the time, Pallas kernels for 5%

profile of v2, /device:TPU:16, one launch (start us, length us, event | category | flops | bytes accessed | tf_op | source)
XLA Modules:
  0.0 23.7 jit_solution(13935757432506513404)
XLA Ops:
  0.6 1.5 %pack.1 = (f32[2,2,64,128]{3,2,1,0:T(8,128)S(1)}, f32[2,2,64,128]{3,2,1,0:T(8,128)S(1)}, f32[3,64,128]{2,1,0:T(8,128)S(1)}, f32[3,64,128]{2,1,0:T(8,128)S(1)}) custom-call(f32[4]{0:T(128)} %scale_hbm.1, f32[2,64,128]{2,1,0:T(8,128)} %perm_log_hbm.1, s32[2,64,128]{2,1,0:T(8,128)} %facies_hbm.1, f32[2,64,128]{2,1,0:T(8,128)} %acc_hbm.1, ...), custom_call_target="tpu_custom_call" | custom-call | tf_op jit(solution)/shard_map/pack/pallas_call | solution.py:572
  2.1 1.6 %collective-permute-start = (f32[3,64,128]{2,1,0:T(8,128)S(1)}, f32[3,64,128]{2,1,0:T(8,128)S(1)}, u32[]{:S(2)}, u32[]{:S(2)}) collective-permute-start(f32[3,64,128]{2,1,0:T(8,128)S(1)} %get-tuple-element.26), channel_id=1, source_target_pairs={{0,1},{1,0},{2,3},{3,2},{4,5},{5,4},{6,7},{7,6},{8,9},{9,8},{10,11... | collective-permute-start | bytes 294920 | tf_op jit(solution)/shard_map/ppermute | solution.py:535
  3.8 1.9 %collective-permute-start.1 = (f32[3,64,128]{2,1,0:T(8,128)S(1)}, f32[3,64,128]{2,1,0:T(8,128)S(1)}, u32[]{:S(2)}, u32[]{:S(2)}) collective-permute-start(f32[3,64,128]{2,1,0:T(8,128)S(1)} %get-tuple-element.27), channel_id=1, source_target_pairs={{1,2},{2,1},{5,6},{6,5},{9,10},{10,9},{13,14},{14,13},{17,18},{18,... | collective-permute-start | bytes 294920 | tf_op jit(solution)/shard_map/ppermute | solution.py:535
  5.7 0.1 collective-permute-start.2
  5.8 0.5 %collective-permute-start.3 = (f32[2,2,64,128]{3,2,1,0:T(8,128)S(1)}, f32[2,2,64,128]{3,2,1,0:T(8,128)S(1)}, u32[]{:S(2)}, u32[]{:S(2)}) collective-permute-start(f32[2,2,64,128]{3,2,1,0:T(8,128)S(1)} %get-tuple-element.25.own_b), channel_id=1, source_target_pairs={{4,0},{0,4},{5,1},{1,5},{6,2},{2,6},{7,3},{3,7},{12,8},{8,12},{13,... | collective-permute-start | bytes 393224 | tf_op jit(solution)/shard_map/ppermute | solution.py:528
  6.3 0.5 %collective-permute-done.message_a = f32[3,64,128]{2,1,0:T(8,128)S(1)} collective-permute-done((f32[3,64,128]{2,1,0:T(8,128)S(1)}, f32[3,64,128]{2,1,0:T(8,128)S(1)}, u32[]{:S(2)}, u32[]{:S(2)}) %collective-permute-start) | collective-permute-done | bytes 98336 | tf_op jit(solution)/shard_map/ppermute | solution.py:535
  6.8 0.0 collective-permute-start.4
  6.8 3.5 %collective-permute-done.1.message_b = f32[3,64,128]{2,1,0:T(8,128)S(1)} collective-permute-done((f32[3,64,128]{2,1,0:T(8,128)S(1)}, f32[3,64,128]{2,1,0:T(8,128)S(1)}, u32[]{:S(2)}, u32[]{:S(2)}) %collective-permute-start.1) | collective-permute-done | bytes 98336 | tf_op jit(solution)/shard_map/ppermute | solution.py:535
  10.3 0.0 collective-permute-start.5
  10.3 0.4 %level_zero.2 = (f32[4,2,2,8,8,128]{5,4,3,2,1,0:T(8,128)S(1)}, f32[2,2,8,8,128]{4,3,2,1,0:T(8,128)S(1)}, f32[2,8,8,128]{3,2,1,0:T(8,128)S(1)}, f32[2,8,8,128]{3,...) custom-call(f32[2,2,64,128]{3,2,1,0:T(8,128)S(1)} %get-tuple-element.24.own_a, ...), custom_call_target="tpu_custom_call" | custom-call | flops 2097152 | bytes 2097152 | tf_op jit(solution)/shard_map/level_zero/pallas_call | solution.py:608
  10.7 0.0 collective-permute-done.2.own_a
  10.7 0.0 collective-permute-done.3.own_b
  10.7 0.0 collective-permute-done.4.message_a
  10.7 0.8 %collective-permute-done.5.message_b = f32[3,64,128]{2,1,0:T(8,128)S(1)} collective-permute-done((f32[3,64,128]{2,1,0:T(8,128)S(1)}, f32[3,64,128]{2,1,0:T(8,128)S(1)}, u32[]{:S(2)}, u32[]{:S(2)}) %collective-permute-start.5) | collective-permute-done | bytes 98336 | tf_op jit(solution)/shard_map/ppermute | solution.py:528
  11.6 0.4 %level_zero.3 = (f32[4,2,2,8,8,128]{5,4,3,2,1,0:T(8,128)S(1)}, f32[2,2,8,8,128]{4,3,2,1,0:T(8,128)S(1)}, f32[2,8,8,128]{3,2,1,0:T(8,128)S(1)}, f32[2,8,8,128]{3,...) custom-call(f32[2,2,64,128]{3,2,1,0:T(8,128)S(1)} %collective-permute-done.2.own_a, ...), custom_call_target="tpu_custom_call" | custom-call | flops 2097152 | bytes 2097152 | tf_op jit(solution)/shard_map/level_zero/pallas_call | solution.py:608
  12.0 3.8 %cycles.1 = (f32[2,64,128]{2,1,0:T(8,128)S(1)}, f32[2,64,128]{2,1,0:T(8,128)S(1)}, f32[2,64,128]{2,1,0:T(8,128)S(1)}) custom-call(s32[1,5]{1,0:T(1,128)} %refs_0_.1, f32[1,5]{1,0:T(1,128)} %refs_1_.1, f32[4,2,2,8,8,128]{5,4,3,2,1,0:T(8,128)S(1)} %get-tuple-element.28.refs_2_, f32[2,2,8,8,128]{4,3,2,1,0:T(8,128)S(1)} %get-tuple-element.29.refs_3_, ...), custom_call_target="tpu_custom_call" | custom-call | tf_op jit(solution)/shard_map/cycles/pallas_call | solution.py:619
  15.8 2.5 %collective-permute-start.8 = (f32[2,64,128]{2,1,0:T(8,128)S(1)}, f32[2,64,128]{2,1,0:T(8,128)S(1)}, u32[]{:S(2)}, u32[]{:S(2)}) collective-permute-start(f32[2,64,128]{2,1,0:T(8,128)S(1)} %get-tuple-element.44), channel_id=1, source_target_pairs={{0,24},{8,16},{16,8},{24,0},{1,25},{9,17},{17,9},{25,1},{2,26},{10... | collective-permute-start | bytes 196616 | tf_op jit(solution)/shard_map/ppermute | solution.py:540
  18.3 0.5 %collective-permute-start.7 = (f32[2,64,128]{2,1,0:T(8,128)S(1)}, f32[2,64,128]{2,1,0:T(8,128)S(1)}, u32[]{:S(2)}, u32[]{:S(2)}) collective-permute-start(f32[2,64,128]{2,1,0:T(8,128)S(1)} %get-tuple-element.44), channel_id=1, source_target_pairs={{0,16},{8,24},{16,0},{24,8},{1,17},{9,25},{17,1},{25,9},{2,18},{10... | collective-permute-start | bytes 196616 | tf_op jit(solution)/shard_map/ppermute | solution.py:540
  18.8 0.5 %collective-permute-start.6 = (f32[2,64,128]{2,1,0:T(8,128)S(1)}, f32[2,64,128]{2,1,0:T(8,128)S(1)}, u32[]{:S(2)}, u32[]{:S(2)}) collective-permute-start(f32[2,64,128]{2,1,0:T(8,128)S(1)} %get-tuple-element.44), channel_id=1, source_target_pairs={{0,8},{8,0},{16,24},{24,16},{1,9},{9,1},{17,25},{25,17},{2,10},{10... | collective-permute-start | bytes 196616 | tf_op jit(solution)/shard_map/ppermute | solution.py:540
  19.3 0.9 %order.1 = (f32[1,2,64,128]{3,2,1,0:T(8,128)}, f32[1,2,64,128]{3,2,1,0:T(8,128)}) custom-call(f32[2,64,128]{2,1,0:T(8,128)S(1)} %get-tuple-element.40.refs_0_, f32[2,64,128]{2,1,0:T(8,128)S(1)} %get-tuple-element.41.refs_1_), custom_call_target="tpu_custom_call" | custom-call | flops 33554432 | bytes 524288 | tf_op jit(solution)/shard_map/order/pallas_call | solution.py:629
  20.2 0.8 %collective-permute-done.8 = f32[2,64,128]{2,1,0:T(8,128)S(1)} collective-permute-done((f32[2,64,128]{2,1,0:T(8,128)S(1)}, f32[2,64,128]{2,1,0:T(8,128)S(1)}, u32[]{:S(2)}, u32[]{:S(2)}) %collective-permute-start.8) | collective-permute-done | bytes 65568 | tf_op jit(solution)/shard_map/ppermute | solution.py:540
  21.0 1.5 %collective-permute-done.7 = f32[2,64,128]{2,1,0:T(8,128)S(1)} collective-permute-done((f32[2,64,128]{2,1,0:T(8,128)S(1)}, f32[2,64,128]{2,1,0:T(8,128)S(1)}, u32[]{:S(2)}, u32[]{:S(2)}) %collective-permute-start.7) | collective-permute-done | bytes 65568 | tf_op jit(solution)/shard_map/ppermute | solution.py:540
  22.6 0.5 %collective-permute-done.6 = f32[2,64,128]{2,1,0:T(8,128)S(1)} collective-permute-done((f32[2,64,128]{2,1,0:T(8,128)S(1)}, f32[2,64,128]{2,1,0:T(8,128)S(1)}, u32[]{:S(2)}, u32[]{:S(2)}) %collective-permute-start.6) | collective-permute-done | bytes 65568 | tf_op jit(solution)/shard_map/ppermute | solution.py:540
  23.1 0.6 %add_add_fusion = f32[2,64,128]{2,1,0:T(8,128)} fusion(f32[2,64,128]{2,1,0:T(8,128)S(1)} %collective-permute-done.7, f32[2,64,128]{2,1,0:T(8,128)S(1)} %collective-permute-done.8, f32[2,64,128]{2,1,0:T(8,128)S(1)} %get-tuple-element.44, f32[2,64,128]{2,1,0:T(8,128)S(1)} %collective-permute-done.6), kind=kLoop, calls=%fused_computation | loop fusion | flops 49152 | bytes 327680 | tf_op jit(solution)/shard_map/add | solution.py:543
Async XLA Ops:
  2.1 4.7 %collective-permute-start = (f32[3,64,128]{2,1,0:T(8,128)S(1)}, f32[3,64,128]{2,1,0:T(8,128)S(1)}, u32[]{:S(2)}, u32[]{:S(2)}) collective-permute-start(f32[3,64,128]{2,1,0:T(8,128)S(1)} %get-tuple-element.26), channel_id=1, source_target_pairs={{0,1},{1,0},{2,3},{3,2},{4,5},{5,4},{6,7},{7,6},{8,9},{9,8},{10,11... | collective-permute-start | bytes 294920 | tf_op jit(solution)/shard_map/ppermute | solution.py:535
  3.8 6.5 %collective-permute-start.1 = (f32[3,64,128]{2,1,0:T(8,128)S(1)}, f32[3,64,128]{2,1,0:T(8,128)S(1)}, u32[]{:S(2)}, u32[]{:S(2)}) collective-permute-start(f32[3,64,128]{2,1,0:T(8,128)S(1)} %get-tuple-element.27), channel_id=1, source_target_pairs={{1,2},{2,1},{5,6},{6,5},{9,10},{10,9},{13,14},{14,13},{17,18},{18,... | collective-permute-start | bytes 294920 | tf_op jit(solution)/shard_map/ppermute | solution.py:535
  5.7 5.0 %collective-permute-start.2 = (f32[2,2,64,128]{3,2,1,0:T(8,128)S(1)}, f32[2,2,64,128]{3,2,1,0:T(8,128)S(1)}, u32[]{:S(2)}, u32[]{:S(2)}) collective-permute-start(f32[2,2,64,128]{3,2,1,0:T(8,128)S(1)} %get-tuple-element.24.own_a), channel_id=1, source_target_pairs={{4,0},{0,4},{5,1},{1,5},{6,2},{2,6},{7,3},{3,7},{12,8},{8,12},{13,... | collective-permute-start | bytes 393224 | tf_op jit(solution)/shard_map/ppermute | solution.py:528
  5.8 4.9 %collective-permute-start.3 = (f32[2,2,64,128]{3,2,1,0:T(8,128)S(1)}, f32[2,2,64,128]{3,2,1,0:T(8,128)S(1)}, u32[]{:S(2)}, u32[]{:S(2)}) collective-permute-start(f32[2,2,64,128]{3,2,1,0:T(8,128)S(1)} %get-tuple-element.25.own_b), channel_id=1, source_target_pairs={{4,0},{0,4},{5,1},{1,5},{6,2},{2,6},{7,3},{3,7},{12,8},{8,12},{13,... | collective-permute-start | bytes 393224 | tf_op jit(solution)/shard_map/ppermute | solution.py:528
  6.8 3.9 %collective-permute-start.4 = (f32[3,64,128]{2,1,0:T(8,128)S(1)}, f32[3,64,128]{2,1,0:T(8,128)S(1)}, u32[]{:S(2)}, u32[]{:S(2)}) collective-permute-start(f32[3,64,128]{2,1,0:T(8,128)S(1)} %collective-permute-done.message_a), channel_id=1, source_target_pairs={{4,0},{0,4},{5,1},{1,5},{6,2},{2,6},{7,3},{3,7},{12,8},{8,12},{13,... | collective-permute-start | bytes 294920 | tf_op jit(solution)/shard_map/ppermute | solution.py:528
  10.3 1.3 %collective-permute-start.5 = (f32[3,64,128]{2,1,0:T(8,128)S(1)}, f32[3,64,128]{2,1,0:T(8,128)S(1)}, u32[]{:S(2)}, u32[]{:S(2)}) collective-permute-start(f32[3,64,128]{2,1,0:T(8,128)S(1)} %collective-permute-done.1.message_b), channel_id=1, source_target_pairs={{4,0},{0,4},{5,1},{1,5},{6,2},{2,6},{7,3},{3,7},{12,8},{8,12},{13,... | collective-permute-start | bytes 294920 | tf_op jit(solution)/shard_map/ppermute | solution.py:528
  15.8 5.3 %collective-permute-start.8 = (f32[2,64,128]{2,1,0:T(8,128)S(1)}, f32[2,64,128]{2,1,0:T(8,128)S(1)}, u32[]{:S(2)}, u32[]{:S(2)}) collective-permute-start(f32[2,64,128]{2,1,0:T(8,128)S(1)} %get-tuple-element.44), channel_id=1, source_target_pairs={{0,24},{8,16},{16,8},{24,0},{1,25},{9,17},{17,9},{25,1},{2,26},{10... | collective-permute-start | bytes 196616 | tf_op jit(solution)/shard_map/ppermute | solution.py:540
  18.3 4.3 %collective-permute-start.7 = (f32[2,64,128]{2,1,0:T(8,128)S(1)}, f32[2,64,128]{2,1,0:T(8,128)S(1)}, u32[]{:S(2)}, u32[]{:S(2)}) collective-permute-start(f32[2,64,128]{2,1,0:T(8,128)S(1)} %get-tuple-element.44), channel_id=1, source_target_pairs={{0,16},{8,24},{16,0},{24,8},{1,17},{9,25},{17,1},{25,9},{2,18},{10... | collective-permute-start | bytes 196616 | tf_op jit(solution)/shard_map/ppermute | solution.py:540
  18.8 4.3 %collective-permute-start.6 = (f32[2,64,128]{2,1,0:T(8,128)S(1)}, f32[2,64,128]{2,1,0:T(8,128)S(1)}, u32[]{:S(2)}, u32[]{:S(2)}) collective-permute-start(f32[2,64,128]{2,1,0:T(8,128)S(1)} %get-tuple-element.44), channel_id=1, source_target_pairs={{0,8},{8,0},{16,24},{24,16},{1,9},{9,1},{17,25},{25,17},{2,10},{10... | collective-permute-start | bytes 196616 | tf_op jit(solution)/shard_map/ppermute | solution.py:540

commit v3 on v1

--- a/solution.py
+++ b/solution.py
@@ -82,22 +82,26 @@
 
 def pack_kernel(scale_hbm, perm_log_hbm, facies_hbm, acc_hbm, prev_hbm, obs_hbm, own_a, own_b, message_a, message_b,
                 scale, perm_log, facies, acc, prev, obs, sems):
-    pairs = ((scale_hbm, scale), (perm_log_hbm, perm_log), (facies_hbm, facies), (acc_hbm, acc), (prev_hbm, prev),
-             (obs_hbm, obs))
+    pairs = ((acc_hbm, acc), (prev_hbm, prev), (obs_hbm, obs), (scale_hbm, scale), (perm_log_hbm, perm_log),
+             (facies_hbm, facies))
     copies = [pltpu.make_async_copy(source, target, sems.at[i]) for i, (source, target) in enumerate(pairs)]
     for copy in copies:
         copy.start()
-    for copy in copies:
-        copy.wait()
 
     def layers(ref):
         return jnp.stack([interleaved(ref.at[layer]) for layer in range(LAYERS)])
 
+    fields = [None]
+    for copy, ref in zip(copies[:3], (acc, prev.at[0], obs.at[0])):
+        copy.wait()
+        fields.append(shuffle(layers(ref), False))
+    for copy in copies[3:]:
+        copy.wait()
     label = layers(facies)
     factor = jnp.zeros(label.shape, jnp.float32)
     for number in range(FACIES):
         factor = factor + jnp.where(label == number, scale[number], jnp.float32(0.0))
-    fields = [shuffle(value, False) for value in (jnp.exp(layers(perm_log)) * factor, layers(acc), layers(prev.at[0]), layers(obs.at[0]))]
+    fields[PERM] = shuffle(jnp.exp(layers(perm_log)) * factor, False)
     for number in range(4):
         (own_a, own_b)[number // 2][number % 2] = fields[number]
     place = place_in_half(label.shape)
@@ -391,6 +395,12 @@
         put_in_order(shuffled[...], ordered.at[0])
 
 
+def split(value, size):
+    if size & (size - 1) == 0:
+        return value >> (size.bit_length() - 1), value & (size - 1)
+    return value // size, value % size
+
+
 def cycle_kernel(grid_shape, blocks, *refs):
     cells_hbm, rates_hbm = refs[:2]
     inputs = [refs[2 + 3 * b:5 + 3 * b] for b in range(blocks)]
@@ -433,15 +443,21 @@
                 finest.now[key] = starts[u]
                 finest.target[key] = accs[u] * starts[u]
 
+    finest_coeffs(finest, perm, joined)
+    with_weight(finest, acc)
+    coarse_coeffs(finest, middle, acc, middle_acc)
+    coarse_coeffs(middle, bottom, middle_acc, bottom_acc)
+
     for copy in copies:
         copy.wait()
     layer_count, total_rows, total_cols = grid_shape
     block_rows, block_cols = SUB * count, LANES
     for well in range(WELLS):
         cell = cells[0, well]
-        layer = cell // (total_rows * total_cols)
-        row = cell // total_cols % total_rows - gx * block_rows
-        col = cell % total_cols - lax.axis_index("gy") * block_cols
+        layer, cell = split(cell, total_rows * total_cols)
+        row, col = split(cell, total_cols)
+        row = row - gx * block_rows
+        col = col - lax.axis_index("gy") * block_cols
         if blocks == 3:
             row_inside = (row >= -block_rows) & (row < 2 * block_rows)
         elif blocks == 2:
@@ -454,15 +470,12 @@
         row = jnp.where(inside, row, 0)
         col = jnp.where(inside, col, 0)
         rate = jnp.where(inside, rates[0, well], 0.0)
-        in_block = row % block_rows
-        place = layer, col % 2, row // block_rows, in_block % count
-        hit = (row_index() == in_block // count) & (lane_index() == col // 2)
+        b, in_block = split(row, block_rows)
+        s, t = split(in_block, count)
+        lane, u = split(col, 2)
+        place = layer, u, b, t
+        hit = (row_index() == s) & (lane_index() == lane)
         finest.target[place] = finest.target[place] + jnp.where(hit, rate, 0.0)
-
-    finest_coeffs(finest, perm, joined)
-    with_weight(finest, acc)
-    coarse_coeffs(finest, middle, acc, middle_acc)
-    coarse_coeffs(middle, bottom, middle_acc, bottom_acc)
 
     sweeps(finest, 1)
     start, other = finest.now, finest.later

time: 23.8 us -> 23.8 us (level)
    pallas_call x1, Pallas kernels: 3.91 us -> 3.61 us  [shards(): pl.pallas_call(partial(cycle_kernel, grid_shape, blocks), out_shape=[pltp...]
    pallas_call x1, Pallas kernels: 1.48 us -> 1.74 us  [shards(): pl.pallas_call(pack_kernel, out_shape=[pltpu.VMEM((2,) + block, f32), plt...]
where the time goes in v3:
time: 23.8 us; the launch traced here: 23.6 us
  waiting for transfers between devices  7.96 us (33%)
  starting transfers between devices  7.68 us (32%)
  Pallas kernels  6.61 us (28%)
  between operations  0.7 us (3%)
  other arithmetic  0.65 us (3%)
    ppermute x2, waiting for transfers between devices, swapped(): return lax.ppermute(value, axis, pairs)  4 us
    pallas_call x1, Pallas kernels, shards(): pl.pallas_call(partial(cycle_kernel, grid_shape, blocks), out_shape=[pltp...  3.61 us
    ppermute x3, starting transfers between devices, summed(): lax.ppermute(value, axis, [(i, i ^ step) for i in range(count)])  3.55 us
    ppermute x2, starting transfers between devices, swapped(): return lax.ppermute(value, axis, pairs)  3.55 us
    ppermute x3, waiting for transfers between devices, summed(): lax.ppermute(value, axis, [(i, i ^ step) for i in range(count)])  2.86 us
    pallas_call x1, Pallas kernels, shards(): pl.pallas_call(pack_kernel, out_shape=[pltpu.VMEM((2,) + block, f32), plt...  1.74 us
    ppermute x4, waiting for transfers between devices, moved(): return lax.ppermute(value, axis, pairs)  1.09 us
    pallas_call x1, Pallas kernels, shards(): pl.pallas_call(order_kernel, out_shape=[state] * 2, in_specs=[vmem] * 2,...  0.87 us
  transfers between devices with their start and end apart: 9, of which 6 were waited for; matrix products, arithmetic and copies ran while one was open for 0% of the time, Pallas kernels for 5%

profile of v3, /device:TPU:16, one launch (start us, length us, event | category | flops | bytes accessed | tf_op | source)
XLA Modules:
  0.0 23.6 jit_solution(13588334355064378712)
XLA Ops:
  0.6 1.7 %pack.1 = (f32[2,2,64,128]{3,2,1,0:T(8,128)S(1)}, f32[2,2,64,128]{3,2,1,0:T(8,128)S(1)}, f32[3,64,128]{2,1,0:T(8,128)S(1)}, f32[3,64,128]{2,1,0:T(8,128)S(1)}) custom-call(f32[4]{0:T(128)} %scale_hbm.1, f32[2,64,128]{2,1,0:T(8,128)} %perm_log_hbm.1, s32[2,64,128]{2,1,0:T(8,128)} %facies_hbm.1, f32[2,64,128]{2,1,0:T(8,128)} %acc_hbm.1, ...), custom_call_target="tpu_custom_call" | custom-call | tf_op jit(solution)/shard_map/pack/pallas_call | solution.py:558
  2.4 1.6 %collective-permute-start = (f32[3,64,128]{2,1,0:T(8,128)S(1)}, f32[3,64,128]{2,1,0:T(8,128)S(1)}, u32[]{:S(2)}, u32[]{:S(2)}) collective-permute-start(f32[3,64,128]{2,1,0:T(8,128)S(1)} %get-tuple-element.14), channel_id=1, source_target_pairs={{0,1},{1,0},{2,3},{3,2},{4,5},{5,4},{6,7},{7,6},{8,9},{9,8},{10,11... | collective-permute-start | bytes 294920 | tf_op jit(solution)/shard_map/ppermute | solution.py:521
  4.0 1.9 %collective-permute-start.1 = (f32[3,64,128]{2,1,0:T(8,128)S(1)}, f32[3,64,128]{2,1,0:T(8,128)S(1)}, u32[]{:S(2)}, u32[]{:S(2)}) collective-permute-start(f32[3,64,128]{2,1,0:T(8,128)S(1)} %get-tuple-element.15), channel_id=1, source_target_pairs={{1,2},{2,1},{5,6},{6,5},{9,10},{10,9},{13,14},{14,13},{17,18},{18,... | collective-permute-start | bytes 294920 | tf_op jit(solution)/shard_map/ppermute | solution.py:521
  5.9 0.1 collective-permute-start.2
  6.0 0.5 %collective-permute-start.3 = (f32[2,2,64,128]{3,2,1,0:T(8,128)S(1)}, f32[2,2,64,128]{3,2,1,0:T(8,128)S(1)}, u32[]{:S(2)}, u32[]{:S(2)}) collective-permute-start(f32[2,2,64,128]{3,2,1,0:T(8,128)S(1)} %get-tuple-element.13.refs_3_), channel_id=1, source_target_pairs={{4,0},{0,4},{5,1},{1,5},{6,2},{2,6},{7,3},{3,7},{12,8},{8,12},{13,... | collective-permute-start | bytes 393224 | tf_op jit(solution)/shard_map/ppermute | solution.py:514
  6.5 0.5 %collective-permute-done.message_a = f32[3,64,128]{2,1,0:T(8,128)S(1)} collective-permute-done((f32[3,64,128]{2,1,0:T(8,128)S(1)}, f32[3,64,128]{2,1,0:T(8,128)S(1)}, u32[]{:S(2)}, u32[]{:S(2)}) %collective-permute-start) | collective-permute-done | bytes 98336 | tf_op jit(solution)/shard_map/ppermute | solution.py:521
  7.1 0.0 collective-permute-start.4
  7.1 3.5 %collective-permute-done.1.message_b = f32[3,64,128]{2,1,0:T(8,128)S(1)} collective-permute-done((f32[3,64,128]{2,1,0:T(8,128)S(1)}, f32[3,64,128]{2,1,0:T(8,128)S(1)}, u32[]{:S(2)}, u32[]{:S(2)}) %collective-permute-start.1) | collective-permute-done | bytes 98336 | tf_op jit(solution)/shard_map/ppermute | solution.py:521
  10.5 0.0 collective-permute-start.5
  10.5 0.2 merge.2.refs_4_
  10.7 0.0 collective-permute-done.4.message_a
  10.7 1.1 %collective-permute-done.5.message_b = f32[3,64,128]{2,1,0:T(8,128)S(1)} collective-permute-done((f32[3,64,128]{2,1,0:T(8,128)S(1)}, f32[3,64,128]{2,1,0:T(8,128)S(1)}, u32[]{:S(2)}, u32[]{:S(2)}) %collective-permute-start.5) | collective-permute-done | bytes 98336 | tf_op jit(solution)/shard_map/ppermute | solution.py:514
  11.8 0.2 merge.3.refs_7_
  12.0 0.0 collective-permute-done.2.refs_5_
  12.0 0.0 collective-permute-done.3.refs_6_
  12.0 3.6 %cycles.1 = (f32[2,64,128]{2,1,0:T(8,128)S(1)}, f32[2,64,128]{2,1,0:T(8,128)S(1)}, f32[2,64,128]{2,1,0:T(8,128)S(1)}) custom-call(s32[1,5]{1,0:T(1,128)} %refs_0_.1, f32[1,5]{1,0:T(1,128)} %refs_1_.1, f32[2,2,64,128]{3,2,1,0:T(8,128)S(1)} %get-tuple-element.12.refs_2_, f32[2,2,64,128]{3,2,1,0:T(8,128)S(1)} %get-tuple-element.13.refs_3_, ...), custom_call_target="tpu_custom_call" | custom-call | tf_op jit(solution)/shard_map/cycles/pallas_call | solution.py:599
  15.7 2.5 %collective-permute-start.8 = (f32[2,64,128]{2,1,0:T(8,128)S(1)}, f32[2,64,128]{2,1,0:T(8,128)S(1)}, u32[]{:S(2)}, u32[]{:S(2)}) collective-permute-start(f32[2,64,128]{2,1,0:T(8,128)S(1)} %get-tuple-element.20), channel_id=1, source_target_pairs={{0,24},{8,16},{16,8},{24,0},{1,25},{9,17},{17,9},{25,1},{2,26},{10... | collective-permute-start | bytes 196616 | tf_op jit(solution)/shard_map/ppermute | solution.py:526
  18.2 0.5 %collective-permute-start.7 = (f32[2,64,128]{2,1,0:T(8,128)S(1)}, f32[2,64,128]{2,1,0:T(8,128)S(1)}, u32[]{:S(2)}, u32[]{:S(2)}) collective-permute-start(f32[2,64,128]{2,1,0:T(8,128)S(1)} %get-tuple-element.20), channel_id=1, source_target_pairs={{0,16},{8,24},{16,0},{24,8},{1,17},{9,25},{17,1},{25,9},{2,18},{10... | collective-permute-start | bytes 196616 | tf_op jit(solution)/shard_map/ppermute | solution.py:526
  18.7 0.5 %collective-permute-start.6 = (f32[2,64,128]{2,1,0:T(8,128)S(1)}, f32[2,64,128]{2,1,0:T(8,128)S(1)}, u32[]{:S(2)}, u32[]{:S(2)}) collective-permute-start(f32[2,64,128]{2,1,0:T(8,128)S(1)} %get-tuple-element.20), channel_id=1, source_target_pairs={{0,8},{8,0},{16,24},{24,16},{1,9},{9,1},{17,25},{25,17},{2,10},{10... | collective-permute-start | bytes 196616 | tf_op jit(solution)/shard_map/ppermute | solution.py:526
  19.2 0.9 %order.1 = (f32[1,2,64,128]{3,2,1,0:T(8,128)}, f32[1,2,64,128]{3,2,1,0:T(8,128)}) custom-call(f32[2,64,128]{2,1,0:T(8,128)S(1)} %get-tuple-element.16.refs_0_, f32[2,64,128]{2,1,0:T(8,128)S(1)} %get-tuple-element.17.refs_1_), custom_call_target="tpu_custom_call" | custom-call | flops 33554432 | bytes 524288 | tf_op jit(solution)/shard_map/order/pallas_call | solution.py:609
  20.1 0.8 %collective-permute-done.8 = f32[2,64,128]{2,1,0:T(8,128)S(1)} collective-permute-done((f32[2,64,128]{2,1,0:T(8,128)S(1)}, f32[2,64,128]{2,1,0:T(8,128)S(1)}, u32[]{:S(2)}, u32[]{:S(2)}) %collective-permute-start.8) | collective-permute-done | bytes 65568 | tf_op jit(solution)/shard_map/ppermute | solution.py:526
  20.9 1.5 %collective-permute-done.7 = f32[2,64,128]{2,1,0:T(8,128)S(1)} collective-permute-done((f32[2,64,128]{2,1,0:T(8,128)S(1)}, f32[2,64,128]{2,1,0:T(8,128)S(1)}, u32[]{:S(2)}, u32[]{:S(2)}) %collective-permute-start.7) | collective-permute-done | bytes 65568 | tf_op jit(solution)/shard_map/ppermute | solution.py:526
  22.4 0.5 %collective-permute-done.6 = f32[2,64,128]{2,1,0:T(8,128)S(1)} collective-permute-done((f32[2,64,128]{2,1,0:T(8,128)S(1)}, f32[2,64,128]{2,1,0:T(8,128)S(1)}, u32[]{:S(2)}, u32[]{:S(2)}) %collective-permute-start.6) | collective-permute-done | bytes 65568 | tf_op jit(solution)/shard_map/ppermute | solution.py:526
  22.9 0.6 %add_add_fusion = f32[2,64,128]{2,1,0:T(8,128)} fusion(f32[2,64,128]{2,1,0:T(8,128)S(1)} %collective-permute-done.7, f32[2,64,128]{2,1,0:T(8,128)S(1)} %collective-permute-done.8, f32[2,64,128]{2,1,0:T(8,128)S(1)} %get-tuple-element.20, f32[2,64,128]{2,1,0:T(8,128)S(1)} %collective-permute-done.6), kind=kLoop, calls=%fused_computation | loop fusion | flops 49152 | bytes 327680 | tf_op jit(solution)/shard_map/add | solution.py:529
Async XLA Ops:
  2.4 4.7 %collective-permute-start = (f32[3,64,128]{2,1,0:T(8,128)S(1)}, f32[3,64,128]{2,1,0:T(8,128)S(1)}, u32[]{:S(2)}, u32[]{:S(2)}) collective-permute-start(f32[3,64,128]{2,1,0:T(8,128)S(1)} %get-tuple-element.14), channel_id=1, source_target_pairs={{0,1},{1,0},{2,3},{3,2},{4,5},{5,4},{6,7},{7,6},{8,9},{9,8},{10,11... | collective-permute-start | bytes 294920 | tf_op jit(solution)/shard_map/ppermute | solution.py:521
  4.0 6.5 %collective-permute-start.1 = (f32[3,64,128]{2,1,0:T(8,128)S(1)}, f32[3,64,128]{2,1,0:T(8,128)S(1)}, u32[]{:S(2)}, u32[]{:S(2)}) collective-permute-start(f32[3,64,128]{2,1,0:T(8,128)S(1)} %get-tuple-element.15), channel_id=1, source_target_pairs={{1,2},{2,1},{5,6},{6,5},{9,10},{10,9},{13,14},{14,13},{17,18},{18,... | collective-permute-start | bytes 294920 | tf_op jit(solution)/shard_map/ppermute | solution.py:521
  5.9 6.1 %collective-permute-start.2 = (f32[2,2,64,128]{3,2,1,0:T(8,128)S(1)}, f32[2,2,64,128]{3,2,1,0:T(8,128)S(1)}, u32[]{:S(2)}, u32[]{:S(2)}) collective-permute-start(f32[2,2,64,128]{3,2,1,0:T(8,128)S(1)} %get-tuple-element.12.refs_2_), channel_id=1, source_target_pairs={{4,0},{0,4},{5,1},{1,5},{6,2},{2,6},{7,3},{3,7},{12,8},{8,12},{13,... | collective-permute-start | bytes 393224 | tf_op jit(solution)/shard_map/ppermute | solution.py:514
  6.0 6.0 %collective-permute-start.3 = (f32[2,2,64,128]{3,2,1,0:T(8,128)S(1)}, f32[2,2,64,128]{3,2,1,0:T(8,128)S(1)}, u32[]{:S(2)}, u32[]{:S(2)}) collective-permute-start(f32[2,2,64,128]{3,2,1,0:T(8,128)S(1)} %get-tuple-element.13.refs_3_), channel_id=1, source_target_pairs={{4,0},{0,4},{5,1},{1,5},{6,2},{2,6},{7,3},{3,7},{12,8},{8,12},{13,... | collective-permute-start | bytes 393224 | tf_op jit(solution)/shard_map/ppermute | solution.py:514
  7.1 3.7 %collective-permute-start.4 = (f32[3,64,128]{2,1,0:T(8,128)S(1)}, f32[3,64,128]{2,1,0:T(8,128)S(1)}, u32[]{:S(2)}, u32[]{:S(2)}) collective-permute-start(f32[3,64,128]{2,1,0:T(8,128)S(1)} %collective-permute-done.message_a), channel_id=1, source_target_pairs={{4,0},{0,4},{5,1},{1,5},{6,2},{2,6},{7,3},{3,7},{12,8},{8,12},{13,... | collective-permute-start | bytes 294920 | tf_op jit(solution)/shard_map/ppermute | solution.py:514
  10.5 1.3 %collective-permute-start.5 = (f32[3,64,128]{2,1,0:T(8,128)S(1)}, f32[3,64,128]{2,1,0:T(8,128)S(1)}, u32[]{:S(2)}, u32[]{:S(2)}) collective-permute-start(f32[3,64,128]{2,1,0:T(8,128)S(1)} %collective-permute-done.1.message_b), channel_id=1, source_target_pairs={{4,0},{0,4},{5,1},{1,5},{6,2},{2,6},{7,3},{3,7},{12,8},{8,12},{13,... | collective-permute-start | bytes 294920 | tf_op jit(solution)/shard_map/ppermute | solution.py:514
  15.7 5.3 %collective-permute-start.8 = (f32[2,64,128]{2,1,0:T(8,128)S(1)}, f32[2,64,128]{2,1,0:T(8,128)S(1)}, u32[]{:S(2)}, u32[]{:S(2)}) collective-permute-start(f32[2,64,128]{2,1,0:T(8,128)S(1)} %get-tuple-element.20), channel_id=1, source_target_pairs={{0,24},{8,16},{16,8},{24,0},{1,25},{9,17},{17,9},{25,1},{2,26},{10... | collective-permute-start | bytes 196616 | tf_op jit(solution)/shard_map/ppermute | solution.py:526
  18.2 4.3 %collective-permute-start.7 = (f32[2,64,128]{2,1,0:T(8,128)S(1)}, f32[2,64,128]{2,1,0:T(8,128)S(1)}, u32[]{:S(2)}, u32[]{:S(2)}) collective-permute-start(f32[2,64,128]{2,1,0:T(8,128)S(1)} %get-tuple-element.20), channel_id=1, source_target_pairs={{0,16},{8,24},{16,0},{24,8},{1,17},{9,25},{17,1},{25,9},{2,18},{10... | collective-permute-start | bytes 196616 | tf_op jit(solution)/shard_map/ppermute | solution.py:526
  18.7 4.3 %collective-permute-start.6 = (f32[2,64,128]{2,1,0:T(8,128)S(1)}, f32[2,64,128]{2,1,0:T(8,128)S(1)}, u32[]{:S(2)}, u32[]{:S(2)}) collective-permute-start(f32[2,64,128]{2,1,0:T(8,128)S(1)} %get-tuple-element.20), channel_id=1, source_target_pairs={{0,8},{8,0},{16,24},{24,16},{1,9},{9,1},{17,25},{25,17},{2,10},{10... | collective-permute-start | bytes 196616 | tf_op jit(solution)/shard_map/ppermute | solution.py:526

commit v4 on v3

--- a/solution.py
+++ b/solution.py
@@ -47,12 +47,13 @@
     natural, place = (cols, rows) if inverse else (rows, cols)
     matrix = (natural == 2 * (place % HALF) + place // HALF).astype(jnp.bfloat16)
     rest = value.reshape(-1, LANES)
-    total = None
+    count = rest.shape[0]
+    parts = []
     for _ in range(3):
-        part = rest.astype(jnp.bfloat16)
-        rest = rest - part.astype(jnp.float32)
-        moved_part = jnp.dot(part, matrix, preferred_element_type=jnp.float32)
-        total = moved_part if total is None else total + moved_part
+        parts.append(rest.astype(jnp.bfloat16))
+        rest = rest - parts[-1].astype(jnp.float32)
+    moved_parts = jnp.dot(jnp.concatenate(parts, 0), matrix, preferred_element_type=jnp.float32)
+    total = moved_parts[:count] + moved_parts[count:2 * count] + moved_parts[2 * count:]
     return total.reshape(value.shape)
 
 
@@ -82,8 +83,8 @@
 
 def pack_kernel(scale_hbm, perm_log_hbm, facies_hbm, acc_hbm, prev_hbm, obs_hbm, own_a, own_b, message_a, message_b,
                 scale, perm_log, facies, acc, prev, obs, sems):
-    pairs = ((acc_hbm, acc), (prev_hbm, prev), (obs_hbm, obs), (scale_hbm, scale), (perm_log_hbm, perm_log),
-             (facies_hbm, facies))
+    pairs = ((scale_hbm, scale), (perm_log_hbm, perm_log), (facies_hbm, facies), (acc_hbm, acc), (prev_hbm, prev),
+             (obs_hbm, obs))
     copies = [pltpu.make_async_copy(source, target, sems.at[i]) for i, (source, target) in enumerate(pairs)]
     for copy in copies:
         copy.start()
@@ -91,17 +92,14 @@
     def layers(ref):
         return jnp.stack([interleaved(ref.at[layer]) for layer in range(LAYERS)])
 
-    fields = [None]
-    for copy, ref in zip(copies[:3], (acc, prev.at[0], obs.at[0])):
-        copy.wait()
-        fields.append(shuffle(layers(ref), False))
-    for copy in copies[3:]:
+    for copy in copies:
         copy.wait()
     label = layers(facies)
     factor = jnp.zeros(label.shape, jnp.float32)
     for number in range(FACIES):
         factor = factor + jnp.where(label == number, scale[number], jnp.float32(0.0))
-    fields[PERM] = shuffle(jnp.exp(layers(perm_log)) * factor, False)
+    fields = shuffle(
+        jnp.stack([jnp.exp(layers(perm_log)) * factor, layers(acc), layers(prev.at[0]), layers(obs.at[0])]), False)
     for number in range(4):
         (own_a, own_b)[number // 2][number % 2] = fields[number]
     place = place_in_half(label.shape)

time: 23.8 us -> 23.6 us (level)
  no operation moved by 1% of the time
where the time goes in v4:
time: 23.6 us; the launch traced here: 23.4 us
  waiting for transfers between devices  7.97 us (34%)
  starting transfers between devices  7.68 us (33%)
  Pallas kernels  6.38 us (27%)
  between operations  0.7 us (3%)
  other arithmetic  0.65 us (3%)
    ppermute x2, waiting for transfers between devices, swapped(): return lax.ppermute(value, axis, pairs)  4 us
    pallas_call x1, Pallas kernels, shards(): pl.pallas_call(partial(cycle_kernel, grid_shape, blocks), out_shape=[pltp...  3.61 us
    ppermute x3, starting transfers between devices, summed(): lax.ppermute(value, axis, [(i, i ^ step) for i in range(count)])  3.55 us
    ppermute x2, starting transfers between devices, swapped(): return lax.ppermute(value, axis, pairs)  3.55 us
    ppermute x3, waiting for transfers between devices, summed(): lax.ppermute(value, axis, [(i, i ^ step) for i in range(count)])  2.87 us
    pallas_call x1, Pallas kernels, shards(): pl.pallas_call(pack_kernel, out_shape=[pltpu.VMEM((2,) + block, f32), plt...  1.52 us
    ppermute x4, waiting for transfers between devices, moved(): return lax.ppermute(value, axis, pairs)  1.09 us
    pallas_call x1, Pallas kernels, shards(): pl.pallas_call(order_kernel, out_shape=[state] * 2, in_specs=[vmem] * 2,...  0.86 us
  transfers between devices with their start and end apart: 9, of which 6 were waited for; matrix products, arithmetic and copies ran while one was open for 0% of the time, Pallas kernels for 5%

profile of v4, /device:TPU:16, one launch (start us, length us, event | category | flops | bytes accessed | tf_op | source)
XLA Modules:
  0.0 23.4 jit_solution(6325524648747180094)
XLA Ops:
  0.6 1.5 %pack.1 = (f32[2,2,64,128]{3,2,1,0:T(8,128)S(1)}, f32[2,2,64,128]{3,2,1,0:T(8,128)S(1)}, f32[3,64,128]{2,1,0:T(8,128)S(1)}, f32[3,64,128]{2,1,0:T(8,128)S(1)}) custom-call(f32[4]{0:T(128)} %scale_hbm.1, f32[2,64,128]{2,1,0:T(8,128)} %perm_log_hbm.1, s32[2,64,128]{2,1,0:T(8,128)} %facies_hbm.1, f32[2,64,128]{2,1,0:T(8,128)} %acc_hbm.1, ...), custom_call_target="tpu_custom_call" | custom-call | tf_op jit(solution)/shard_map/pack/pallas_call | solution.py:556
  2.2 1.6 %collective-permute-start = (f32[3,64,128]{2,1,0:T(8,128)S(1)}, f32[3,64,128]{2,1,0:T(8,128)S(1)}, u32[]{:S(2)}, u32[]{:S(2)}) collective-permute-start(f32[3,64,128]{2,1,0:T(8,128)S(1)} %get-tuple-element.14), channel_id=1, source_target_pairs={{0,1},{1,0},{2,3},{3,2},{4,5},{5,4},{6,7},{7,6},{8,9},{9,8},{10,11... | collective-permute-start | bytes 294920 | tf_op jit(solution)/shard_map/ppermute | solution.py:519
  3.8 1.9 %collective-permute-start.1 = (f32[3,64,128]{2,1,0:T(8,128)S(1)}, f32[3,64,128]{2,1,0:T(8,128)S(1)}, u32[]{:S(2)}, u32[]{:S(2)}) collective-permute-start(f32[3,64,128]{2,1,0:T(8,128)S(1)} %get-tuple-element.15), channel_id=1, source_target_pairs={{1,2},{2,1},{5,6},{6,5},{9,10},{10,9},{13,14},{14,13},{17,18},{18,... | collective-permute-start | bytes 294920 | tf_op jit(solution)/shard_map/ppermute | solution.py:519
  5.7 0.1 collective-permute-start.2
  5.8 0.5 %collective-permute-start.3 = (f32[2,2,64,128]{3,2,1,0:T(8,128)S(1)}, f32[2,2,64,128]{3,2,1,0:T(8,128)S(1)}, u32[]{:S(2)}, u32[]{:S(2)}) collective-permute-start(f32[2,2,64,128]{3,2,1,0:T(8,128)S(1)} %get-tuple-element.13.refs_3_), channel_id=1, source_target_pairs={{4,0},{0,4},{5,1},{1,5},{6,2},{2,6},{7,3},{3,7},{12,8},{8,12},{13,... | collective-permute-start | bytes 393224 | tf_op jit(solution)/shard_map/ppermute | solution.py:512
  6.3 0.5 %collective-permute-done.message_a = f32[3,64,128]{2,1,0:T(8,128)S(1)} collective-permute-done((f32[3,64,128]{2,1,0:T(8,128)S(1)}, f32[3,64,128]{2,1,0:T(8,128)S(1)}, u32[]{:S(2)}, u32[]{:S(2)}) %collective-permute-start) | collective-permute-done | bytes 98336 | tf_op jit(solution)/shard_map/ppermute | solution.py:519
  6.8 0.0 collective-permute-start.4
  6.8 3.5 %collective-permute-done.1.message_b = f32[3,64,128]{2,1,0:T(8,128)S(1)} collective-permute-done((f32[3,64,128]{2,1,0:T(8,128)S(1)}, f32[3,64,128]{2,1,0:T(8,128)S(1)}, u32[]{:S(2)}, u32[]{:S(2)}) %collective-permute-start.1) | collective-permute-done | bytes 98336 | tf_op jit(solution)/shard_map/ppermute | solution.py:519
  10.3 0.0 collective-permute-start.5
  10.3 0.2 merge.2.refs_4_
  10.5 0.0 collective-permute-done.4.message_a
  10.5 1.1 %collective-permute-done.5.message_b = f32[3,64,128]{2,1,0:T(8,128)S(1)} collective-permute-done((f32[3,64,128]{2,1,0:T(8,128)S(1)}, f32[3,64,128]{2,1,0:T(8,128)S(1)}, u32[]{:S(2)}, u32[]{:S(2)}) %collective-permute-start.5) | collective-permute-done | bytes 98336 | tf_op jit(solution)/shard_map/ppermute | solution.py:512
  11.6 0.2 merge.3.refs_7_
  11.8 0.0 collective-permute-done.2.refs_5_
  11.8 0.0 collective-permute-done.3.refs_6_
  11.8 3.6 %cycles.1 = (f32[2,64,128]{2,1,0:T(8,128)S(1)}, f32[2,64,128]{2,1,0:T(8,128)S(1)}, f32[2,64,128]{2,1,0:T(8,128)S(1)}) custom-call(s32[1,5]{1,0:T(1,128)} %refs_0_.1, f32[1,5]{1,0:T(1,128)} %refs_1_.1, f32[2,2,64,128]{3,2,1,0:T(8,128)S(1)} %get-tuple-element.12.refs_2_, f32[2,2,64,128]{3,2,1,0:T(8,128)S(1)} %get-tuple-element.13.refs_3_, ...), custom_call_target="tpu_custom_call" | custom-call | tf_op jit(solution)/shard_map/cycles/pallas_call | solution.py:597
  15.4 2.5 %collective-permute-start.8 = (f32[2,64,128]{2,1,0:T(8,128)S(1)}, f32[2,64,128]{2,1,0:T(8,128)S(1)}, u32[]{:S(2)}, u32[]{:S(2)}) collective-permute-start(f32[2,64,128]{2,1,0:T(8,128)S(1)} %get-tuple-element.20), channel_id=1, source_target_pairs={{0,24},{8,16},{16,8},{24,0},{1,25},{9,17},{17,9},{25,1},{2,26},{10... | collective-permute-start | bytes 196616 | tf_op jit(solution)/shard_map/ppermute | solution.py:524
  18.0 0.5 %collective-permute-start.7 = (f32[2,64,128]{2,1,0:T(8,128)S(1)}, f32[2,64,128]{2,1,0:T(8,128)S(1)}, u32[]{:S(2)}, u32[]{:S(2)}) collective-permute-start(f32[2,64,128]{2,1,0:T(8,128)S(1)} %get-tuple-element.20), channel_id=1, source_target_pairs={{0,16},{8,24},{16,0},{24,8},{1,17},{9,25},{17,1},{25,9},{2,18},{10... | collective-permute-start | bytes 196616 | tf_op jit(solution)/shard_map/ppermute | solution.py:524
  18.5 0.5 %collective-permute-start.6 = (f32[2,64,128]{2,1,0:T(8,128)S(1)}, f32[2,64,128]{2,1,0:T(8,128)S(1)}, u32[]{:S(2)}, u32[]{:S(2)}) collective-permute-start(f32[2,64,128]{2,1,0:T(8,128)S(1)} %get-tuple-element.20), channel_id=1, source_target_pairs={{0,8},{8,0},{16,24},{24,16},{1,9},{9,1},{17,25},{25,17},{2,10},{10... | collective-permute-start | bytes 196616 | tf_op jit(solution)/shard_map/ppermute | solution.py:524
  19.0 0.9 %order.1 = (f32[1,2,64,128]{3,2,1,0:T(8,128)}, f32[1,2,64,128]{3,2,1,0:T(8,128)}) custom-call(f32[2,64,128]{2,1,0:T(8,128)S(1)} %get-tuple-element.16.refs_0_, f32[2,64,128]{2,1,0:T(8,128)S(1)} %get-tuple-element.17.refs_1_), custom_call_target="tpu_custom_call" | custom-call | flops 33554432 | bytes 524288 | tf_op jit(solution)/shard_map/order/pallas_call | solution.py:607
  19.9 0.8 %collective-permute-done.8 = f32[2,64,128]{2,1,0:T(8,128)S(1)} collective-permute-done((f32[2,64,128]{2,1,0:T(8,128)S(1)}, f32[2,64,128]{2,1,0:T(8,128)S(1)}, u32[]{:S(2)}, u32[]{:S(2)}) %collective-permute-start.8) | collective-permute-done | bytes 65568 | tf_op jit(solution)/shard_map/ppermute | solution.py:524
  20.7 1.5 %collective-permute-done.7 = f32[2,64,128]{2,1,0:T(8,128)S(1)} collective-permute-done((f32[2,64,128]{2,1,0:T(8,128)S(1)}, f32[2,64,128]{2,1,0:T(8,128)S(1)}, u32[]{:S(2)}, u32[]{:S(2)}) %collective-permute-start.7) | collective-permute-done | bytes 65568 | tf_op jit(solution)/shard_map/ppermute | solution.py:524
  22.2 0.5 %collective-permute-done.6 = f32[2,64,128]{2,1,0:T(8,128)S(1)} collective-permute-done((f32[2,64,128]{2,1,0:T(8,128)S(1)}, f32[2,64,128]{2,1,0:T(8,128)S(1)}, u32[]{:S(2)}, u32[]{:S(2)}) %collective-permute-start.6) | collective-permute-done | bytes 65568 | tf_op jit(solution)/shard_map/ppermute | solution.py:524
  22.7 0.6 %add_add_fusion = f32[2,64,128]{2,1,0:T(8,128)} fusion(f32[2,64,128]{2,1,0:T(8,128)S(1)} %collective-permute-done.7, f32[2,64,128]{2,1,0:T(8,128)S(1)} %collective-permute-done.8, f32[2,64,128]{2,1,0:T(8,128)S(1)} %get-tuple-element.20, f32[2,64,128]{2,1,0:T(8,128)S(1)} %collective-permute-done.6), kind=kLoop, calls=%fused_computation | loop fusion | flops 49152 | bytes 327680 | tf_op jit(solution)/shard_map/add | solution.py:527
Async XLA Ops:
  2.2 4.7 %collective-permute-start = (f32[3,64,128]{2,1,0:T(8,128)S(1)}, f32[3,64,128]{2,1,0:T(8,128)S(1)}, u32[]{:S(2)}, u32[]{:S(2)}) collective-permute-start(f32[3,64,128]{2,1,0:T(8,128)S(1)} %get-tuple-element.14), channel_id=1, source_target_pairs={{0,1},{1,0},{2,3},{3,2},{4,5},{5,4},{6,7},{7,6},{8,9},{9,8},{10,11... | collective-permute-start | bytes 294920 | tf_op jit(solution)/shard_map/ppermute | solution.py:519
  3.8 6.5 %collective-permute-start.1 = (f32[3,64,128]{2,1,0:T(8,128)S(1)}, f32[3,64,128]{2,1,0:T(8,128)S(1)}, u32[]{:S(2)}, u32[]{:S(2)}) collective-permute-start(f32[3,64,128]{2,1,0:T(8,128)S(1)} %get-tuple-element.15), channel_id=1, source_target_pairs={{1,2},{2,1},{5,6},{6,5},{9,10},{10,9},{13,14},{14,13},{17,18},{18,... | collective-permute-start | bytes 294920 | tf_op jit(solution)/shard_map/ppermute | solution.py:519
  5.7 6.1 %collective-permute-start.2 = (f32[2,2,64,128]{3,2,1,0:T(8,128)S(1)}, f32[2,2,64,128]{3,2,1,0:T(8,128)S(1)}, u32[]{:S(2)}, u32[]{:S(2)}) collective-permute-start(f32[2,2,64,128]{3,2,1,0:T(8,128)S(1)} %get-tuple-element.12.refs_2_), channel_id=1, source_target_pairs={{4,0},{0,4},{5,1},{1,5},{6,2},{2,6},{7,3},{3,7},{12,8},{8,12},{13,... | collective-permute-start | bytes 393224 | tf_op jit(solution)/shard_map/ppermute | solution.py:512
  5.8 6.0 %collective-permute-start.3 = (f32[2,2,64,128]{3,2,1,0:T(8,128)S(1)}, f32[2,2,64,128]{3,2,1,0:T(8,128)S(1)}, u32[]{:S(2)}, u32[]{:S(2)}) collective-permute-start(f32[2,2,64,128]{3,2,1,0:T(8,128)S(1)} %get-tuple-element.13.refs_3_), channel_id=1, source_target_pairs={{4,0},{0,4},{5,1},{1,5},{6,2},{2,6},{7,3},{3,7},{12,8},{8,12},{13,... | collective-permute-start | bytes 393224 | tf_op jit(solution)/shard_map/ppermute | solution.py:512
  6.8 3.7 %collective-permute-start.4 = (f32[3,64,128]{2,1,0:T(8,128)S(1)}, f32[3,64,128]{2,1,0:T(8,128)S(1)}, u32[]{:S(2)}, u32[]{:S(2)}) collective-permute-start(f32[3,64,128]{2,1,0:T(8,128)S(1)} %collective-permute-done.message_a), channel_id=1, source_target_pairs={{4,0},{0,4},{5,1},{1,5},{6,2},{2,6},{7,3},{3,7},{12,8},{8,12},{13,... | collective-permute-start | bytes 294920 | tf_op jit(solution)/shard_map/ppermute | solution.py:512
  10.3 1.3 %collective-permute-start.5 = (f32[3,64,128]{2,1,0:T(8,128)S(1)}, f32[3,64,128]{2,1,0:T(8,128)S(1)}, u32[]{:S(2)}, u32[]{:S(2)}) collective-permute-start(f32[3,64,128]{2,1,0:T(8,128)S(1)} %collective-permute-done.1.message_b), channel_id=1, source_target_pairs={{4,0},{0,4},{5,1},{1,5},{6,2},{2,6},{7,3},{3,7},{12,8},{8,12},{13,... | collective-permute-start | bytes 294920 | tf_op jit(solution)/shard_map/ppermute | solution.py:512
  15.4 5.3 %collective-permute-start.8 = (f32[2,64,128]{2,1,0:T(8,128)S(1)}, f32[2,64,128]{2,1,0:T(8,128)S(1)}, u32[]{:S(2)}, u32[]{:S(2)}) collective-permute-start(f32[2,64,128]{2,1,0:T(8,128)S(1)} %get-tuple-element.20), channel_id=1, source_target_pairs={{0,24},{8,16},{16,8},{24,0},{1,25},{9,17},{17,9},{25,1},{2,26},{10... | collective-permute-start | bytes 196616 | tf_op jit(solution)/shard_map/ppermute | solution.py:524
  18.0 4.3 %collective-permute-start.7 = (f32[2,64,128]{2,1,0:T(8,128)S(1)}, f32[2,64,128]{2,1,0:T(8,128)S(1)}, u32[]{:S(2)}, u32[]{:S(2)}) collective-permute-start(f32[2,64,128]{2,1,0:T(8,128)S(1)} %get-tuple-element.20), channel_id=1, source_target_pairs={{0,16},{8,24},{16,0},{24,8},{1,17},{9,25},{17,1},{25,9},{2,18},{10... | collective-permute-start | bytes 196616 | tf_op jit(solution)/shard_map/ppermute | solution.py:524
  18.5 4.3 %collective-permute-start.6 = (f32[2,64,128]{2,1,0:T(8,128)S(1)}, f32[2,64,128]{2,1,0:T(8,128)S(1)}, u32[]{:S(2)}, u32[]{:S(2)}) collective-permute-start(f32[2,64,128]{2,1,0:T(8,128)S(1)} %get-tuple-element.20), channel_id=1, source_target_pairs={{0,8},{8,0},{16,24},{24,16},{1,9},{9,1},{17,25},{25,17},{2,10},{10... | collective-permute-start | bytes 196616 | tf_op jit(solution)/shard_map/ppermute | solution.py:524
